TPU v7x, 512 devices: a whole 4x4x16 slice. The times are simulated.
512 devices in a mesh: tm: 16 (over x_hi, y, core), space: 32 (over z, x_lo).
Axes of the slice: x: 4 (x_hi: 2, x_lo: 2; x = x_hi * 2 + x_lo), y: 4, z: 16, core: 2. Of those that a mesh axis runs over, the one named last changes fastest.
Arguments:
- initial_states: float32 [16, 64, 32, 256], P('tm', 'space'), may hold values from -6 to 6
- velocity: float32 [3, 64, 32, 256], P(None, 'space'), may hold values from -2 to 2
- diffusivity: float32 [64, 32, 256], P('space'), may hold values from 0.005 to 0.05
Outputs:
- new_ends: float32 [16, 64, 32, 256], P('tm', 'space')
All inputs are finite; a program needn't handle non-finite values.
Results may differ from a plain program's by a relative error of at most 0.00002.
Values sent between devices are 32-bit elements; how exact they have to be, the bound alone decides.
A program may use at most 64 MiB of HBM per device.

v0:
```python
import jax
import jax.numpy as jnp
from jax import lax
from jax.sharding import PartitionSpec as P

FINE_STEPS = 2


def with_halo(shard, sides, width):
    for axis, dim in sides:
        peers, length = (lax.axis_size(axis), shard.shape[dim])
        up = [(i, (i + 1) % peers) for i in range(peers - 1)]
        down = [(j, i) for i, j in up]
        last = lax.slice_in_dim(shard, length - width, length, axis=dim)
        leading = lax.slice_in_dim(shard, 0, width, axis=dim)
        before = lax.ppermute(last, axis, up)
        after = lax.ppermute(leading, axis, down)
        shard = jnp.concatenate([before, shard, after], axis=dim)
    return shard


def passed_along(shard, axis, by):
    peers = lax.axis_size(axis)
    pairs = [(i, i + by) for i in range(peers) if 0 <= i + by < peers]
    return lax.ppermute(shard, axis, pairs)


def restrict(field):
    leading = field.shape[:-3]
    shaped = field.reshape(
        leading + (field.shape[-3] // 2, 2, field.shape[-2] // 2, 2, field.shape[-1] // 2, 2)
    )
    return jnp.mean(shaped, axis=(-5, -3, -1))


def prolong(field):
    return jnp.repeat(jnp.repeat(jnp.repeat(field, 2, axis=-3), 2, axis=-2), 2, axis=-1)


def advance(extended, diffusivity, velocity, spread):
    padded = jnp.pad(extended, ((0, 0), (1, 1), (1, 1)))
    center = padded[1:-1, 1:-1, 1:-1]
    x_plus = padded[2:, 1:-1, 1:-1]
    x_minus = padded[:-2, 1:-1, 1:-1]
    y_plus = padded[1:-1, 2:, 1:-1]
    y_minus = padded[1:-1, :-2, 1:-1]
    z_plus = padded[1:-1, 1:-1, 2:]
    z_minus = padded[1:-1, 1:-1, :-2]
    laplace = (
        x_plus
        + x_minus
        - 2.0 * center
        + (y_plus + y_minus - 2.0 * center)
        + (z_plus + z_minus - 2.0 * center)
    )
    drift_term = (
        velocity[0] * (x_plus - x_minus)
        + velocity[1] * (y_plus - y_minus)
        + velocity[2] * (z_plus - z_minus)
    )
    return center + spread * diffusivity * laplace - 0.5 * drift_term


def shards(initial_states, velocity, diffusivity):
    fine_field = initial_states[0]
    for section in range(FINE_STEPS):
        extended = with_halo(fine_field, (("space", 0),), 1)
        fine_field = advance(extended, diffusivity, velocity, 1.0)
    coarse_diffusivity = restrict(diffusivity)
    coarse_velocity = restrict(velocity)

    def coarse(field):
        extended_coarse = with_halo(field, (("space", 0),), 1)
        return advance(extended_coarse, coarse_diffusivity, coarse_velocity, 0.5)

    coarse_start = restrict(initial_states[0])
    coarse_end = restrict(fine_field)
    correction = coarse_end - coarse(coarse_start)
    position = lax.axis_index("tm")
    slices = lax.axis_size("tm")

    def relay_step(turn, carried):
        incoming = passed_along(carried, "tm", 1)
        source = jnp.where(position == 0, coarse_start, incoming)
        return coarse(source) + correction

    coarse_chain = lax.fori_loop(0, slices, relay_step, jnp.zeros_like(coarse_start))
    new_end = fine_field + prolong(coarse_chain - coarse_end)
    return new_end[None]


def solution(mesh):
    in_specs = (P("tm", "space", None, None), P(None, "space", None, None), P("space", None, None))
    out_specs = P("tm", "space", None, None)
    return jax.shard_map(shards, mesh=mesh, in_specs=in_specs, out_specs=out_specs, check_vma=False)
```

profile of v0, /device:TPU:388, one launch (start us, length us, event | category | flops | bytes accessed | tf_op | source)
XLA Modules:
  0.0 342.1 jit_solution(9530271444445463658)
XLA Ops:
  3.3 4.8 %collective-permute-start.7 = (f32[1,16,128]{2,1,0:T(8,128)S(1)}, f32[1,16,128]{2,1,0:T(8,128)S(1)}, u32[]{:S(2)}, u32[]{:S(2)}) collective-permute-start(f32[1,16,128]{2,1,0:T(8,128)S(1)} %multiply_bitcast_fusion.1), channel_id=1, source_target_pairs={{1,0},{2,1},{3,2},{4,3},{5,4},{6,5},{7,6},{8,7},{9,8},{10,9},{11,1... | collective-permute-start | bytes 24584 | tf_op jit(solution)/shard_map/ppermute | solution.py:17
  10.0 6.0 %collective-permute-start.3 = (f32[1,32,256]{2,1,0:T(8,128)S(1)}, f32[1,32,256]{2,1,0:T(8,128)S(1)}, u32[]{:S(2)}, u32[]{:S(2)}) collective-permute-start(f32[1,32,256]{2,1,0:T(8,128)S(1)} %get-tuple-element.163), channel_id=1, source_target_pairs={{1,0},{2,1},{3,2},{4,3},{5,4},{6,5},{7,6},{8,7},{9,8},{10,9},{11,1... | collective-permute-start | bytes 98312 | tf_op jit(solution)/shard_map/ppermute | solution.py:17
  18.0 7.6 %reduce_sum.59 = f32[3,16,2,128,2]{4,3,2,1,0:T(8,128)} reshape(f32[3,32,256]{2,1,0:T(8,128)S(1)} %reduce_sum.55) | data formatting | bytes 196608 | tf_op jit(solution)/shard_map/reduce_sum | solution.py:33
  29.8 6.0 %collective-permute-start.5 = (f32[1,32,256]{2,1,0:T(8,128)S(1)}, f32[1,32,256]{2,1,0:T(8,128)S(1)}, u32[]{:S(2)}, u32[]{:S(2)}) collective-permute-start(f32[1,32,256]{2,1,0:T(8,128)S(1)} %get-tuple-element.161), channel_id=1, source_target_pairs={{1,0},{2,1},{3,2},{4,3},{5,4},{6,5},{7,6},{8,7},{9,8},{10,9},{11,1... | collective-permute-start | bytes 98312 | tf_op jit(solution)/shard_map/ppermute | solution.py:17
  46.6 294.5 %while.13 = (s32[]{:T(128)}, f32[1,16,128]{2,1,0:T(8,128)S(1)}, pred[]{:T(512)}, f32[1,16,128]{2,1,0:T(8,128)S(1)}, f32[1,16,128]{2,1,0:T(8,128)S(1)}, /*index=5...) while((s32[]{:T(128)}, f32[1,16,128]{2,1,0:T(8,128)S(1)}, ...), condition=%wide.region_9.10_spmd.clone, body=%wide.region_8.9_spmd.clone.sunk | while | flops 156503 | bytes 298640 | solution.py:87
  48.6 6.7 %collective-permute-done = f32[1,16,128]{2,1,0:T(8,128)S(1)} collective-permute-done((f32[1,16,128]{2,1,0:T(8,128)S(1)}, f32[1,16,128]{2,1,0:T(8,128)S(1)}, u32[]{:S(2)}, u32[]{:S(2)}) %collective-permute-start) | collective-permute-done | bytes 8224 | tf_op jit(solution)/shard_map/while/body/eval_jaxpr/ppermute | solution.py:25
  61.1 4.3 %collective-permute-done.2 = f32[1,16,128]{2,1,0:T(8,128)S(1)} collective-permute-done((f32[1,16,128]{2,1,0:T(8,128)S(1)}, f32[1,16,128]{2,1,0:T(8,128)S(1)}, u32[]{:S(2)}, u32[]{:S(2)}) %collective-permute-start.2) | collective-permute-done | bytes 8224 | tf_op jit(solution)/shard_map/while/body/eval_jaxpr/ppermute | solution.py:16
  67.5 6.7 %collective-permute-done = f32[1,16,128]{2,1,0:T(8,128)S(1)} collective-permute-done((f32[1,16,128]{2,1,0:T(8,128)S(1)}, f32[1,16,128]{2,1,0:T(8,128)S(1)}, u32[]{:S(2)}, u32[]{:S(2)}) %collective-permute-start) | collective-permute-done | bytes 8224 | tf_op jit(solution)/shard_map/while/body/eval_jaxpr/ppermute | solution.py:25
  76.1 3.9 %collective-permute-start.2 = (f32[1,16,128]{2,1,0:T(8,128)S(1)}, f32[1,16,128]{2,1,0:T(8,128)S(1)}, u32[]{:S(2)}, u32[]{:S(2)}) collective-permute-start(f32[1,16,128]{2,1,0:T(8,128)S(1)} %broadcast_select_fusion.5), channel_id=1, source_target_pairs={{0,1},{1,2},{2,3},{3,4},{4,5},{5,6},{6,7},{7,8},{8,9},{9,10},{10,1... | collective-permute-start | bytes 24584 | tf_op jit(solution)/shard_map/while/body/eval_jaxpr/ppermute | solution.py:16
  80.1 3.7 %collective-permute-done.2 = f32[1,16,128]{2,1,0:T(8,128)S(1)} collective-permute-done((f32[1,16,128]{2,1,0:T(8,128)S(1)}, f32[1,16,128]{2,1,0:T(8,128)S(1)}, u32[]{:S(2)}, u32[]{:S(2)}) %collective-permute-start.2) | collective-permute-done | bytes 8224 | tf_op jit(solution)/shard_map/while/body/eval_jaxpr/ppermute | solution.py:16
  85.9 6.7 %collective-permute-done = f32[1,16,128]{2,1,0:T(8,128)S(1)} collective-permute-done((f32[1,16,128]{2,1,0:T(8,128)S(1)}, f32[1,16,128]{2,1,0:T(8,128)S(1)}, u32[]{:S(2)}, u32[]{:S(2)}) %collective-permute-start) | collective-permute-done | bytes 8224 | tf_op jit(solution)/shard_map/while/body/eval_jaxpr/ppermute | solution.py:25
  94.5 3.9 %collective-permute-start.2 = (f32[1,16,128]{2,1,0:T(8,128)S(1)}, f32[1,16,128]{2,1,0:T(8,128)S(1)}, u32[]{:S(2)}, u32[]{:S(2)}) collective-permute-start(f32[1,16,128]{2,1,0:T(8,128)S(1)} %broadcast_select_fusion.5), channel_id=1, source_target_pairs={{0,1},{1,2},{2,3},{3,4},{4,5},{5,6},{6,7},{7,8},{8,9},{9,10},{10,1... | collective-permute-start | bytes 24584 | tf_op jit(solution)/shard_map/while/body/eval_jaxpr/ppermute | solution.py:16
  98.4 3.7 %collective-permute-done.2 = f32[1,16,128]{2,1,0:T(8,128)S(1)} collective-permute-done((f32[1,16,128]{2,1,0:T(8,128)S(1)}, f32[1,16,128]{2,1,0:T(8,128)S(1)}, u32[]{:S(2)}, u32[]{:S(2)}) %collective-permute-start.2) | collective-permute-done | bytes 8224 | tf_op jit(solution)/shard_map/while/body/eval_jaxpr/ppermute | solution.py:16
  104.3 6.7 %collective-permute-done = f32[1,16,128]{2,1,0:T(8,128)S(1)} collective-permute-done((f32[1,16,128]{2,1,0:T(8,128)S(1)}, f32[1,16,128]{2,1,0:T(8,128)S(1)}, u32[]{:S(2)}, u32[]{:S(2)}) %collective-permute-start) | collective-permute-done | bytes 8224 | tf_op jit(solution)/shard_map/while/body/eval_jaxpr/ppermute | solution.py:25
  112.9 3.9 %collective-permute-start.2 = (f32[1,16,128]{2,1,0:T(8,128)S(1)}, f32[1,16,128]{2,1,0:T(8,128)S(1)}, u32[]{:S(2)}, u32[]{:S(2)}) collective-permute-start(f32[1,16,128]{2,1,0:T(8,128)S(1)} %broadcast_select_fusion.5), channel_id=1, source_target_pairs={{0,1},{1,2},{2,3},{3,4},{4,5},{5,6},{6,7},{7,8},{8,9},{9,10},{10,1... | collective-permute-start | bytes 24584 | tf_op jit(solution)/shard_map/while/body/eval_jaxpr/ppermute | solution.py:16
  116.8 3.7 %collective-permute-done.2 = f32[1,16,128]{2,1,0:T(8,128)S(1)} collective-permute-done((f32[1,16,128]{2,1,0:T(8,128)S(1)}, f32[1,16,128]{2,1,0:T(8,128)S(1)}, u32[]{:S(2)}, u32[]{:S(2)}) %collective-permute-start.2) | collective-permute-done | bytes 8224 | tf_op jit(solution)/shard_map/while/body/eval_jaxpr/ppermute | solution.py:16
  122.7 6.7 %collective-permute-done = f32[1,16,128]{2,1,0:T(8,128)S(1)} collective-permute-done((f32[1,16,128]{2,1,0:T(8,128)S(1)}, f32[1,16,128]{2,1,0:T(8,128)S(1)}, u32[]{:S(2)}, u32[]{:S(2)}) %collective-permute-start) | collective-permute-done | bytes 8224 | tf_op jit(solution)/shard_map/while/body/eval_jaxpr/ppermute | solution.py:25
  131.2 3.9 %collective-permute-start.2 = (f32[1,16,128]{2,1,0:T(8,128)S(1)}, f32[1,16,128]{2,1,0:T(8,128)S(1)}, u32[]{:S(2)}, u32[]{:S(2)}) collective-permute-start(f32[1,16,128]{2,1,0:T(8,128)S(1)} %broadcast_select_fusion.5), channel_id=1, source_target_pairs={{0,1},{1,2},{2,3},{3,4},{4,5},{5,6},{6,7},{7,8},{8,9},{9,10},{10,1... | collective-permute-start | bytes 24584 | tf_op jit(solution)/shard_map/while/body/eval_jaxpr/ppermute | solution.py:16
  135.2 3.7 %collective-permute-done.2 = f32[1,16,128]{2,1,0:T(8,128)S(1)} collective-permute-done((f32[1,16,128]{2,1,0:T(8,128)S(1)}, f32[1,16,128]{2,1,0:T(8,128)S(1)}, u32[]{:S(2)}, u32[]{:S(2)}) %collective-permute-start.2) | collective-permute-done | bytes 8224 | tf_op jit(solution)/shard_map/while/body/eval_jaxpr/ppermute | solution.py:16
  141.0 6.7 %collective-permute-done = f32[1,16,128]{2,1,0:T(8,128)S(1)} collective-permute-done((f32[1,16,128]{2,1,0:T(8,128)S(1)}, f32[1,16,128]{2,1,0:T(8,128)S(1)}, u32[]{:S(2)}, u32[]{:S(2)}) %collective-permute-start) | collective-permute-done | bytes 8224 | tf_op jit(solution)/shard_map/while/body/eval_jaxpr/ppermute | solution.py:25
  149.6 3.9 %collective-permute-start.2 = (f32[1,16,128]{2,1,0:T(8,128)S(1)}, f32[1,16,128]{2,1,0:T(8,128)S(1)}, u32[]{:S(2)}, u32[]{:S(2)}) collective-permute-start(f32[1,16,128]{2,1,0:T(8,128)S(1)} %broadcast_select_fusion.5), channel_id=1, source_target_pairs={{0,1},{1,2},{2,3},{3,4},{4,5},{5,6},{6,7},{7,8},{8,9},{9,10},{10,1... | collective-permute-start | bytes 24584 | tf_op jit(solution)/shard_map/while/body/eval_jaxpr/ppermute | solution.py:16
  153.5 3.7 %collective-permute-done.2 = f32[1,16,128]{2,1,0:T(8,128)S(1)} collective-permute-done((f32[1,16,128]{2,1,0:T(8,128)S(1)}, f32[1,16,128]{2,1,0:T(8,128)S(1)}, u32[]{:S(2)}, u32[]{:S(2)}) %collective-permute-start.2) | collective-permute-done | bytes 8224 | tf_op jit(solution)/shard_map/while/body/eval_jaxpr/ppermute | solution.py:16
  159.4 6.7 %collective-permute-done = f32[1,16,128]{2,1,0:T(8,128)S(1)} collective-permute-done((f32[1,16,128]{2,1,0:T(8,128)S(1)}, f32[1,16,128]{2,1,0:T(8,128)S(1)}, u32[]{:S(2)}, u32[]{:S(2)}) %collective-permute-start) | collective-permute-done | bytes 8224 | tf_op jit(solution)/shard_map/while/body/eval_jaxpr/ppermute | solution.py:25
  168.0 3.9 %collective-permute-start.2 = (f32[1,16,128]{2,1,0:T(8,128)S(1)}, f32[1,16,128]{2,1,0:T(8,128)S(1)}, u32[]{:S(2)}, u32[]{:S(2)}) collective-permute-start(f32[1,16,128]{2,1,0:T(8,128)S(1)} %broadcast_select_fusion.5), channel_id=1, source_target_pairs={{0,1},{1,2},{2,3},{3,4},{4,5},{5,6},{6,7},{7,8},{8,9},{9,10},{10,1... | collective-permute-start | bytes 24584 | tf_op jit(solution)/shard_map/while/body/eval_jaxpr/ppermute | solution.py:16
  171.9 3.7 %collective-permute-done.2 = f32[1,16,128]{2,1,0:T(8,128)S(1)} collective-permute-done((f32[1,16,128]{2,1,0:T(8,128)S(1)}, f32[1,16,128]{2,1,0:T(8,128)S(1)}, u32[]{:S(2)}, u32[]{:S(2)}) %collective-permute-start.2) | collective-permute-done | bytes 8224 | tf_op jit(solution)/shard_map/while/body/eval_jaxpr/ppermute | solution.py:16
  177.8 6.7 %collective-permute-done = f32[1,16,128]{2,1,0:T(8,128)S(1)} collective-permute-done((f32[1,16,128]{2,1,0:T(8,128)S(1)}, f32[1,16,128]{2,1,0:T(8,128)S(1)}, u32[]{:S(2)}, u32[]{:S(2)}) %collective-permute-start) | collective-permute-done | bytes 8224 | tf_op jit(solution)/shard_map/while/body/eval_jaxpr/ppermute | solution.py:25
  186.3 3.9 %collective-permute-start.2 = (f32[1,16,128]{2,1,0:T(8,128)S(1)}, f32[1,16,128]{2,1,0:T(8,128)S(1)}, u32[]{:S(2)}, u32[]{:S(2)}) collective-permute-start(f32[1,16,128]{2,1,0:T(8,128)S(1)} %broadcast_select_fusion.5), channel_id=1, source_target_pairs={{0,1},{1,2},{2,3},{3,4},{4,5},{5,6},{6,7},{7,8},{8,9},{9,10},{10,1... | collective-permute-start | bytes 24584 | tf_op jit(solution)/shard_map/while/body/eval_jaxpr/ppermute | solution.py:16
  190.3 3.7 %collective-permute-done.2 = f32[1,16,128]{2,1,0:T(8,128)S(1)} collective-permute-done((f32[1,16,128]{2,1,0:T(8,128)S(1)}, f32[1,16,128]{2,1,0:T(8,128)S(1)}, u32[]{:S(2)}, u32[]{:S(2)}) %collective-permute-start.2) | collective-permute-done | bytes 8224 | tf_op jit(solution)/shard_map/while/body/eval_jaxpr/ppermute | solution.py:16
  196.1 6.7 %collective-permute-done = f32[1,16,128]{2,1,0:T(8,128)S(1)} collective-permute-done((f32[1,16,128]{2,1,0:T(8,128)S(1)}, f32[1,16,128]{2,1,0:T(8,128)S(1)}, u32[]{:S(2)}, u32[]{:S(2)}) %collective-permute-start) | collective-permute-done | bytes 8224 | tf_op jit(solution)/shard_map/while/body/eval_jaxpr/ppermute | solution.py:25
  204.7 3.9 %collective-permute-start.2 = (f32[1,16,128]{2,1,0:T(8,128)S(1)}, f32[1,16,128]{2,1,0:T(8,128)S(1)}, u32[]{:S(2)}, u32[]{:S(2)}) collective-permute-start(f32[1,16,128]{2,1,0:T(8,128)S(1)} %broadcast_select_fusion.5), channel_id=1, source_target_pairs={{0,1},{1,2},{2,3},{3,4},{4,5},{5,6},{6,7},{7,8},{8,9},{9,10},{10,1... | collective-permute-start | bytes 24584 | tf_op jit(solution)/shard_map/while/body/eval_jaxpr/ppermute | solution.py:16
  208.7 3.7 %collective-permute-done.2 = f32[1,16,128]{2,1,0:T(8,128)S(1)} collective-permute-done((f32[1,16,128]{2,1,0:T(8,128)S(1)}, f32[1,16,128]{2,1,0:T(8,128)S(1)}, u32[]{:S(2)}, u32[]{:S(2)}) %collective-permute-start.2) | collective-permute-done | bytes 8224 | tf_op jit(solution)/shard_map/while/body/eval_jaxpr/ppermute | solution.py:16
  214.5 6.7 %collective-permute-done = f32[1,16,128]{2,1,0:T(8,128)S(1)} collective-permute-done((f32[1,16,128]{2,1,0:T(8,128)S(1)}, f32[1,16,128]{2,1,0:T(8,128)S(1)}, u32[]{:S(2)}, u32[]{:S(2)}) %collective-permute-start) | collective-permute-done | bytes 8224 | tf_op jit(solution)/shard_map/while/body/eval_jaxpr/ppermute | solution.py:25
  223.1 3.9 %collective-permute-start.2 = (f32[1,16,128]{2,1,0:T(8,128)S(1)}, f32[1,16,128]{2,1,0:T(8,128)S(1)}, u32[]{:S(2)}, u32[]{:S(2)}) collective-permute-start(f32[1,16,128]{2,1,0:T(8,128)S(1)} %broadcast_select_fusion.5), channel_id=1, source_target_pairs={{0,1},{1,2},{2,3},{3,4},{4,5},{5,6},{6,7},{7,8},{8,9},{9,10},{10,1... | collective-permute-start | bytes 24584 | tf_op jit(solution)/shard_map/while/body/eval_jaxpr/ppermute | solution.py:16
  227.0 3.7 %collective-permute-done.2 = f32[1,16,128]{2,1,0:T(8,128)S(1)} collective-permute-done((f32[1,16,128]{2,1,0:T(8,128)S(1)}, f32[1,16,128]{2,1,0:T(8,128)S(1)}, u32[]{:S(2)}, u32[]{:S(2)}) %collective-permute-start.2) | collective-permute-done | bytes 8224 | tf_op jit(solution)/shard_map/while/body/eval_jaxpr/ppermute | solution.py:16
  232.9 6.7 %collective-permute-done = f32[1,16,128]{2,1,0:T(8,128)S(1)} collective-permute-done((f32[1,16,128]{2,1,0:T(8,128)S(1)}, f32[1,16,128]{2,1,0:T(8,128)S(1)}, u32[]{:S(2)}, u32[]{:S(2)}) %collective-permute-start) | collective-permute-done | bytes 8224 | tf_op jit(solution)/shard_map/while/body/eval_jaxpr/ppermute | solution.py:25
  241.5 3.9 %collective-permute-start.2 = (f32[1,16,128]{2,1,0:T(8,128)S(1)}, f32[1,16,128]{2,1,0:T(8,128)S(1)}, u32[]{:S(2)}, u32[]{:S(2)}) collective-permute-start(f32[1,16,128]{2,1,0:T(8,128)S(1)} %broadcast_select_fusion.5), channel_id=1, source_target_pairs={{0,1},{1,2},{2,3},{3,4},{4,5},{5,6},{6,7},{7,8},{8,9},{9,10},{10,1... | collective-permute-start | bytes 24584 | tf_op jit(solution)/shard_map/while/body/eval_jaxpr/ppermute | solution.py:16
  251.3 6.7 %collective-permute-done = f32[1,16,128]{2,1,0:T(8,128)S(1)} collective-permute-done((f32[1,16,128]{2,1,0:T(8,128)S(1)}, f32[1,16,128]{2,1,0:T(8,128)S(1)}, u32[]{:S(2)}, u32[]{:S(2)}) %collective-permute-start) | collective-permute-done | bytes 8224 | tf_op jit(solution)/shard_map/while/body/eval_jaxpr/ppermute | solution.py:25
  259.8 3.9 %collective-permute-start.2 = (f32[1,16,128]{2,1,0:T(8,128)S(1)}, f32[1,16,128]{2,1,0:T(8,128)S(1)}, u32[]{:S(2)}, u32[]{:S(2)}) collective-permute-start(f32[1,16,128]{2,1,0:T(8,128)S(1)} %broadcast_select_fusion.5), channel_id=1, source_target_pairs={{0,1},{1,2},{2,3},{3,4},{4,5},{5,6},{6,7},{7,8},{8,9},{9,10},{10,1... | collective-permute-start | bytes 24584 | tf_op jit(solution)/shard_map/while/body/eval_jaxpr/ppermute | solution.py:16
  263.8 3.7 %collective-permute-done.2 = f32[1,16,128]{2,1,0:T(8,128)S(1)} collective-permute-done((f32[1,16,128]{2,1,0:T(8,128)S(1)}, f32[1,16,128]{2,1,0:T(8,128)S(1)}, u32[]{:S(2)}, u32[]{:S(2)}) %collective-permute-start.2) | collective-permute-done | bytes 8224 | tf_op jit(solution)/shard_map/while/body/eval_jaxpr/ppermute | solution.py:16
  269.6 6.7 %collective-permute-done = f32[1,16,128]{2,1,0:T(8,128)S(1)} collective-permute-done((f32[1,16,128]{2,1,0:T(8,128)S(1)}, f32[1,16,128]{2,1,0:T(8,128)S(1)}, u32[]{:S(2)}, u32[]{:S(2)}) %collective-permute-start) | collective-permute-done | bytes 8224 | tf_op jit(solution)/shard_map/while/body/eval_jaxpr/ppermute | solution.py:25
  278.2 3.9 %collective-permute-start.2 = (f32[1,16,128]{2,1,0:T(8,128)S(1)}, f32[1,16,128]{2,1,0:T(8,128)S(1)}, u32[]{:S(2)}, u32[]{:S(2)}) collective-permute-start(f32[1,16,128]{2,1,0:T(8,128)S(1)} %broadcast_select_fusion.5), channel_id=1, source_target_pairs={{0,1},{1,2},{2,3},{3,4},{4,5},{5,6},{6,7},{7,8},{8,9},{9,10},{10,1... | collective-permute-start | bytes 24584 | tf_op jit(solution)/shard_map/while/body/eval_jaxpr/ppermute | solution.py:16
  288.0 6.7 %collective-permute-done = f32[1,16,128]{2,1,0:T(8,128)S(1)} collective-permute-done((f32[1,16,128]{2,1,0:T(8,128)S(1)}, f32[1,16,128]{2,1,0:T(8,128)S(1)}, u32[]{:S(2)}, u32[]{:S(2)}) %collective-permute-start) | collective-permute-done | bytes 8224 | tf_op jit(solution)/shard_map/while/body/eval_jaxpr/ppermute | solution.py:25
  296.6 3.9 %collective-permute-start.2 = (f32[1,16,128]{2,1,0:T(8,128)S(1)}, f32[1,16,128]{2,1,0:T(8,128)S(1)}, u32[]{:S(2)}, u32[]{:S(2)}) collective-permute-start(f32[1,16,128]{2,1,0:T(8,128)S(1)} %broadcast_select_fusion.5), channel_id=1, source_target_pairs={{0,1},{1,2},{2,3},{3,4},{4,5},{5,6},{6,7},{7,8},{8,9},{9,10},{10,1... | collective-permute-start | bytes 24584 | tf_op jit(solution)/shard_map/while/body/eval_jaxpr/ppermute | solution.py:16
  306.4 6.7 %collective-permute-done = f32[1,16,128]{2,1,0:T(8,128)S(1)} collective-permute-done((f32[1,16,128]{2,1,0:T(8,128)S(1)}, f32[1,16,128]{2,1,0:T(8,128)S(1)}, u32[]{:S(2)}, u32[]{:S(2)}) %collective-permute-start) | collective-permute-done | bytes 8224 | tf_op jit(solution)/shard_map/while/body/eval_jaxpr/ppermute | solution.py:25
  314.9 3.9 %collective-permute-start.2 = (f32[1,16,128]{2,1,0:T(8,128)S(1)}, f32[1,16,128]{2,1,0:T(8,128)S(1)}, u32[]{:S(2)}, u32[]{:S(2)}) collective-permute-start(f32[1,16,128]{2,1,0:T(8,128)S(1)} %broadcast_select_fusion.5), channel_id=1, source_target_pairs={{0,1},{1,2},{2,3},{3,4},{4,5},{5,6},{6,7},{7,8},{8,9},{9,10},{10,1... | collective-permute-start | bytes 24584 | tf_op jit(solution)/shard_map/while/body/eval_jaxpr/ppermute | solution.py:16
  324.7 6.7 %collective-permute-done = f32[1,16,128]{2,1,0:T(8,128)S(1)} collective-permute-done((f32[1,16,128]{2,1,0:T(8,128)S(1)}, f32[1,16,128]{2,1,0:T(8,128)S(1)}, u32[]{:S(2)}, u32[]{:S(2)}) %collective-permute-start) | collective-permute-done | bytes 8224 | tf_op jit(solution)/shard_map/while/body/eval_jaxpr/ppermute | solution.py:25
  333.3 3.9 %collective-permute-start.2 = (f32[1,16,128]{2,1,0:T(8,128)S(1)}, f32[1,16,128]{2,1,0:T(8,128)S(1)}, u32[]{:S(2)}, u32[]{:S(2)}) collective-permute-start(f32[1,16,128]{2,1,0:T(8,128)S(1)} %broadcast_select_fusion.5), channel_id=1, source_target_pairs={{0,1},{1,2},{2,3},{3,4},{4,5},{5,6},{6,7},{7,8},{8,9},{9,10},{10,1... | collective-permute-start | bytes 24584 | tf_op jit(solution)/shard_map/while/body/eval_jaxpr/ppermute | solution.py:16
  337.3 3.7 %collective-permute-done.2 = f32[1,16,128]{2,1,0:T(8,128)S(1)} collective-permute-done((f32[1,16,128]{2,1,0:T(8,128)S(1)}, f32[1,16,128]{2,1,0:T(8,128)S(1)}, u32[]{:S(2)}, u32[]{:S(2)}) %collective-permute-start.2) | collective-permute-done | bytes 8224 | tf_op jit(solution)/shard_map/while/body/eval_jaxpr/ppermute | solution.py:16
  (159 shorter events, 105.7 us)
Async XLA Ops:
  3.3 26.1 %collective-permute-start.7 = (f32[1,16,128]{2,1,0:T(8,128)S(1)}, f32[1,16,128]{2,1,0:T(8,128)S(1)}, u32[]{:S(2)}, u32[]{:S(2)}) collective-permute-start(f32[1,16,128]{2,1,0:T(8,128)S(1)} %multiply_bitcast_fusion.1), channel_id=1, source_target_pairs={{1,0},{2,1},{3,2},{4,3},{5,4},{6,5},{7,6},{8,7},{9,8},{10,9},{11,1... | collective-permute-start | bytes 24584 | tf_op jit(solution)/shard_map/ppermute | solution.py:17
  8.1 21.3 %collective-permute-start.8 = (f32[1,16,128]{2,1,0:T(8,128)S(1)}, f32[1,16,128]{2,1,0:T(8,128)S(1)}, u32[]{:S(2)}, u32[]{:S(2)}) collective-permute-start(f32[1,16,128]{2,1,0:T(8,128)S(1)} %multiply_bitcast_fusion.1), channel_id=1, source_target_pairs={{0,1},{1,2},{2,3},{3,4},{4,5},{5,6},{6,7},{7,8},{8,9},{9,10},{10,1... | collective-permute-start | bytes 24584 | tf_op jit(solution)/shard_map/ppermute | solution.py:16
  10.0 19.5 %collective-permute-start.3 = (f32[1,32,256]{2,1,0:T(8,128)S(1)}, f32[1,32,256]{2,1,0:T(8,128)S(1)}, u32[]{:S(2)}, u32[]{:S(2)}) collective-permute-start(f32[1,32,256]{2,1,0:T(8,128)S(1)} %get-tuple-element.163), channel_id=1, source_target_pairs={{1,0},{2,1},{3,2},{4,3},{5,4},{6,5},{7,6},{8,7},{9,8},{10,9},{11,1... | collective-permute-start | bytes 98312 | tf_op jit(solution)/shard_map/ppermute | solution.py:17
  16.1 13.5 %collective-permute-start.4 = (f32[1,32,256]{2,1,0:T(8,128)S(1)}, f32[1,32,256]{2,1,0:T(8,128)S(1)}, u32[]{:S(2)}, u32[]{:S(2)}) collective-permute-start(f32[1,32,256]{2,1,0:T(8,128)S(1)} %get-tuple-element.162), channel_id=1, source_target_pairs={{0,1},{1,2},{2,3},{3,4},{4,5},{5,6},{6,7},{7,8},{8,9},{9,10},{10,1... | collective-permute-start | bytes 98312 | tf_op jit(solution)/shard_map/ppermute | solution.py:16
  29.8 10.4 %collective-permute-start.5 = (f32[1,32,256]{2,1,0:T(8,128)S(1)}, f32[1,32,256]{2,1,0:T(8,128)S(1)}, u32[]{:S(2)}, u32[]{:S(2)}) collective-permute-start(f32[1,32,256]{2,1,0:T(8,128)S(1)} %get-tuple-element.161), channel_id=1, source_target_pairs={{1,0},{2,1},{3,2},{4,3},{5,4},{6,5},{7,6},{8,7},{9,8},{10,9},{11,1... | collective-permute-start | bytes 98312 | tf_op jit(solution)/shard_map/ppermute | solution.py:17
  35.9 7.9 %collective-permute-start.6 = (f32[1,32,256]{2,1,0:T(8,128)S(1)}, f32[1,32,256]{2,1,0:T(8,128)S(1)}, u32[]{:S(2)}, u32[]{:S(2)}) collective-permute-start(f32[1,32,256]{2,1,0:T(8,128)S(1)} %get-tuple-element.160), channel_id=1, source_target_pairs={{0,1},{1,2},{2,3},{3,4},{4,5},{5,6},{6,7},{7,8},{8,9},{9,10},{10,1... | collective-permute-start | bytes 98312 | tf_op jit(solution)/shard_map/ppermute | solution.py:16
  46.6 8.6 %collective-permute-start = (f32[1,16,128]{2,1,0:T(8,128)S(1)}, f32[1,16,128]{2,1,0:T(8,128)S(1)}, u32[]{:S(2)}, u32[]{:S(2)}) collective-permute-start(f32[1,16,128]{2,1,0:T(8,128)S(1)} %broadcast_select_fusion.4), channel_id=1, source_target_pairs={{0,32},{32,64},{64,96},{96,128},{128,160},{160,192},{192,224},{224... | collective-permute-start | bytes 24584 | tf_op jit(solution)/shard_map/while/body/eval_jaxpr/ppermute | solution.py:25
  57.7 7.7 %collective-permute-start.2 = (f32[1,16,128]{2,1,0:T(8,128)S(1)}, f32[1,16,128]{2,1,0:T(8,128)S(1)}, u32[]{:S(2)}, u32[]{:S(2)}) collective-permute-start(f32[1,16,128]{2,1,0:T(8,128)S(1)} %broadcast_select_fusion.5), channel_id=1, source_target_pairs={{0,1},{1,2},{2,3},{3,4},{4,5},{5,6},{6,7},{7,8},{8,9},{9,10},{10,1... | collective-permute-start | bytes 24584 | tf_op jit(solution)/shard_map/while/body/eval_jaxpr/ppermute | solution.py:16
  65.6 8.6 %collective-permute-start = (f32[1,16,128]{2,1,0:T(8,128)S(1)}, f32[1,16,128]{2,1,0:T(8,128)S(1)}, u32[]{:S(2)}, u32[]{:S(2)}) collective-permute-start(f32[1,16,128]{2,1,0:T(8,128)S(1)} %broadcast_select_fusion.4), channel_id=1, source_target_pairs={{0,32},{32,64},{64,96},{96,128},{128,160},{160,192},{192,224},{224... | collective-permute-start | bytes 24584 | tf_op jit(solution)/shard_map/while/body/eval_jaxpr/ppermute | solution.py:25
  74.2 5.8 %collective-permute-start.1 = (f32[1,16,128]{2,1,0:T(8,128)S(1)}, f32[1,16,128]{2,1,0:T(8,128)S(1)}, u32[]{:S(2)}, u32[]{:S(2)}) collective-permute-start(f32[1,16,128]{2,1,0:T(8,128)S(1)} %broadcast_select_fusion.5), channel_id=1, source_target_pairs={{1,0},{2,1},{3,2},{4,3},{5,4},{6,5},{7,6},{8,7},{9,8},{10,9},{11,1... | collective-permute-start | bytes 24584 | tf_op jit(solution)/shard_map/while/body/eval_jaxpr/ppermute | solution.py:17
  76.1 7.7 %collective-permute-start.2 = (f32[1,16,128]{2,1,0:T(8,128)S(1)}, f32[1,16,128]{2,1,0:T(8,128)S(1)}, u32[]{:S(2)}, u32[]{:S(2)}) collective-permute-start(f32[1,16,128]{2,1,0:T(8,128)S(1)} %broadcast_select_fusion.5), channel_id=1, source_target_pairs={{0,1},{1,2},{2,3},{3,4},{4,5},{5,6},{6,7},{7,8},{8,9},{9,10},{10,1... | collective-permute-start | bytes 24584 | tf_op jit(solution)/shard_map/while/body/eval_jaxpr/ppermute | solution.py:16
  84.0 8.6 %collective-permute-start = (f32[1,16,128]{2,1,0:T(8,128)S(1)}, f32[1,16,128]{2,1,0:T(8,128)S(1)}, u32[]{:S(2)}, u32[]{:S(2)}) collective-permute-start(f32[1,16,128]{2,1,0:T(8,128)S(1)} %broadcast_select_fusion.4), channel_id=1, source_target_pairs={{0,32},{32,64},{64,96},{96,128},{128,160},{160,192},{192,224},{224... | collective-permute-start | bytes 24584 | tf_op jit(solution)/shard_map/while/body/eval_jaxpr/ppermute | solution.py:25
  94.5 7.7 %collective-permute-start.2 = (f32[1,16,128]{2,1,0:T(8,128)S(1)}, f32[1,16,128]{2,1,0:T(8,128)S(1)}, u32[]{:S(2)}, u32[]{:S(2)}) collective-permute-start(f32[1,16,128]{2,1,0:T(8,128)S(1)} %broadcast_select_fusion.5), channel_id=1, source_target_pairs={{0,1},{1,2},{2,3},{3,4},{4,5},{5,6},{6,7},{7,8},{8,9},{9,10},{10,1... | collective-permute-start | bytes 24584 | tf_op jit(solution)/shard_map/while/body/eval_jaxpr/ppermute | solution.py:16
  102.4 8.6 %collective-permute-start = (f32[1,16,128]{2,1,0:T(8,128)S(1)}, f32[1,16,128]{2,1,0:T(8,128)S(1)}, u32[]{:S(2)}, u32[]{:S(2)}) collective-permute-start(f32[1,16,128]{2,1,0:T(8,128)S(1)} %broadcast_select_fusion.4), channel_id=1, source_target_pairs={{0,32},{32,64},{64,96},{96,128},{128,160},{160,192},{192,224},{224... | collective-permute-start | bytes 24584 | tf_op jit(solution)/shard_map/while/body/eval_jaxpr/ppermute | solution.py:25
  110.9 5.8 %collective-permute-start.1 = (f32[1,16,128]{2,1,0:T(8,128)S(1)}, f32[1,16,128]{2,1,0:T(8,128)S(1)}, u32[]{:S(2)}, u32[]{:S(2)}) collective-permute-start(f32[1,16,128]{2,1,0:T(8,128)S(1)} %broadcast_select_fusion.5), channel_id=1, source_target_pairs={{1,0},{2,1},{3,2},{4,3},{5,4},{6,5},{7,6},{8,7},{9,8},{10,9},{11,1... | collective-permute-start | bytes 24584 | tf_op jit(solution)/shard_map/while/body/eval_jaxpr/ppermute | solution.py:17
  112.9 7.7 %collective-permute-start.2 = (f32[1,16,128]{2,1,0:T(8,128)S(1)}, f32[1,16,128]{2,1,0:T(8,128)S(1)}, u32[]{:S(2)}, u32[]{:S(2)}) collective-permute-start(f32[1,16,128]{2,1,0:T(8,128)S(1)} %broadcast_select_fusion.5), channel_id=1, source_target_pairs={{0,1},{1,2},{2,3},{3,4},{4,5},{5,6},{6,7},{7,8},{8,9},{9,10},{10,1... | collective-permute-start | bytes 24584 | tf_op jit(solution)/shard_map/while/body/eval_jaxpr/ppermute | solution.py:16
  120.7 8.6 %collective-permute-start = (f32[1,16,128]{2,1,0:T(8,128)S(1)}, f32[1,16,128]{2,1,0:T(8,128)S(1)}, u32[]{:S(2)}, u32[]{:S(2)}) collective-permute-start(f32[1,16,128]{2,1,0:T(8,128)S(1)} %broadcast_select_fusion.4), channel_id=1, source_target_pairs={{0,32},{32,64},{64,96},{96,128},{128,160},{160,192},{192,224},{224... | collective-permute-start | bytes 24584 | tf_op jit(solution)/shard_map/while/body/eval_jaxpr/ppermute | solution.py:25
  129.3 5.8 %collective-permute-start.1 = (f32[1,16,128]{2,1,0:T(8,128)S(1)}, f32[1,16,128]{2,1,0:T(8,128)S(1)}, u32[]{:S(2)}, u32[]{:S(2)}) collective-permute-start(f32[1,16,128]{2,1,0:T(8,128)S(1)} %broadcast_select_fusion.5), channel_id=1, source_target_pairs={{1,0},{2,1},{3,2},{4,3},{5,4},{6,5},{7,6},{8,7},{9,8},{10,9},{11,1... | collective-permute-start | bytes 24584 | tf_op jit(solution)/shard_map/while/body/eval_jaxpr/ppermute | solution.py:17
  131.2 7.7 %collective-permute-start.2 = (f32[1,16,128]{2,1,0:T(8,128)S(1)}, f32[1,16,128]{2,1,0:T(8,128)S(1)}, u32[]{:S(2)}, u32[]{:S(2)}) collective-permute-start(f32[1,16,128]{2,1,0:T(8,128)S(1)} %broadcast_select_fusion.5), channel_id=1, source_target_pairs={{0,1},{1,2},{2,3},{3,4},{4,5},{5,6},{6,7},{7,8},{8,9},{9,10},{10,1... | collective-permute-start | bytes 24584 | tf_op jit(solution)/shard_map/while/body/eval_jaxpr/ppermute | solution.py:16
  139.1 8.6 %collective-permute-start = (f32[1,16,128]{2,1,0:T(8,128)S(1)}, f32[1,16,128]{2,1,0:T(8,128)S(1)}, u32[]{:S(2)}, u32[]{:S(2)}) collective-permute-start(f32[1,16,128]{2,1,0:T(8,128)S(1)} %broadcast_select_fusion.4), channel_id=1, source_target_pairs={{0,32},{32,64},{64,96},{96,128},{128,160},{160,192},{192,224},{224... | collective-permute-start | bytes 24584 | tf_op jit(solution)/shard_map/while/body/eval_jaxpr/ppermute | solution.py:25
  147.7 5.8 %collective-permute-start.1 = (f32[1,16,128]{2,1,0:T(8,128)S(1)}, f32[1,16,128]{2,1,0:T(8,128)S(1)}, u32[]{:S(2)}, u32[]{:S(2)}) collective-permute-start(f32[1,16,128]{2,1,0:T(8,128)S(1)} %broadcast_select_fusion.5), channel_id=1, source_target_pairs={{1,0},{2,1},{3,2},{4,3},{5,4},{6,5},{7,6},{8,7},{9,8},{10,9},{11,1... | collective-permute-start | bytes 24584 | tf_op jit(solution)/shard_map/while/body/eval_jaxpr/ppermute | solution.py:17
  149.6 7.7 %collective-permute-start.2 = (f32[1,16,128]{2,1,0:T(8,128)S(1)}, f32[1,16,128]{2,1,0:T(8,128)S(1)}, u32[]{:S(2)}, u32[]{:S(2)}) collective-permute-start(f32[1,16,128]{2,1,0:T(8,128)S(1)} %broadcast_select_fusion.5), channel_id=1, source_target_pairs={{0,1},{1,2},{2,3},{3,4},{4,5},{5,6},{6,7},{7,8},{8,9},{9,10},{10,1... | collective-permute-start | bytes 24584 | tf_op jit(solution)/shard_map/while/body/eval_jaxpr/ppermute | solution.py:16
  157.5 8.6 %collective-permute-start = (f32[1,16,128]{2,1,0:T(8,128)S(1)}, f32[1,16,128]{2,1,0:T(8,128)S(1)}, u32[]{:S(2)}, u32[]{:S(2)}) collective-permute-start(f32[1,16,128]{2,1,0:T(8,128)S(1)} %broadcast_select_fusion.4), channel_id=1, source_target_pairs={{0,32},{32,64},{64,96},{96,128},{128,160},{160,192},{192,224},{224... | collective-permute-start | bytes 24584 | tf_op jit(solution)/shard_map/while/body/eval_jaxpr/ppermute | solution.py:25
  168.0 7.7 %collective-permute-start.2 = (f32[1,16,128]{2,1,0:T(8,128)S(1)}, f32[1,16,128]{2,1,0:T(8,128)S(1)}, u32[]{:S(2)}, u32[]{:S(2)}) collective-permute-start(f32[1,16,128]{2,1,0:T(8,128)S(1)} %broadcast_select_fusion.5), channel_id=1, source_target_pairs={{0,1},{1,2},{2,3},{3,4},{4,5},{5,6},{6,7},{7,8},{8,9},{9,10},{10,1... | collective-permute-start | bytes 24584 | tf_op jit(solution)/shard_map/while/body/eval_jaxpr/ppermute | solution.py:16
  175.8 8.6 %collective-permute-start = (f32[1,16,128]{2,1,0:T(8,128)S(1)}, f32[1,16,128]{2,1,0:T(8,128)S(1)}, u32[]{:S(2)}, u32[]{:S(2)}) collective-permute-start(f32[1,16,128]{2,1,0:T(8,128)S(1)} %broadcast_select_fusion.4), channel_id=1, source_target_pairs={{0,32},{32,64},{64,96},{96,128},{128,160},{160,192},{192,224},{224... | collective-permute-start | bytes 24584 | tf_op jit(solution)/shard_map/while/body/eval_jaxpr/ppermute | solution.py:25
  184.4 5.8 %collective-permute-start.1 = (f32[1,16,128]{2,1,0:T(8,128)S(1)}, f32[1,16,128]{2,1,0:T(8,128)S(1)}, u32[]{:S(2)}, u32[]{:S(2)}) collective-permute-start(f32[1,16,128]{2,1,0:T(8,128)S(1)} %broadcast_select_fusion.5), channel_id=1, source_target_pairs={{1,0},{2,1},{3,2},{4,3},{5,4},{6,5},{7,6},{8,7},{9,8},{10,9},{11,1... | collective-permute-start | bytes 24584 | tf_op jit(solution)/shard_map/while/body/eval_jaxpr/ppermute | solution.py:17
  186.3 7.7 %collective-permute-start.2 = (f32[1,16,128]{2,1,0:T(8,128)S(1)}, f32[1,16,128]{2,1,0:T(8,128)S(1)}, u32[]{:S(2)}, u32[]{:S(2)}) collective-permute-start(f32[1,16,128]{2,1,0:T(8,128)S(1)} %broadcast_select_fusion.5), channel_id=1, source_target_pairs={{0,1},{1,2},{2,3},{3,4},{4,5},{5,6},{6,7},{7,8},{8,9},{9,10},{10,1... | collective-permute-start | bytes 24584 | tf_op jit(solution)/shard_map/while/body/eval_jaxpr/ppermute | solution.py:16
  194.2 8.6 %collective-permute-start = (f32[1,16,128]{2,1,0:T(8,128)S(1)}, f32[1,16,128]{2,1,0:T(8,128)S(1)}, u32[]{:S(2)}, u32[]{:S(2)}) collective-permute-start(f32[1,16,128]{2,1,0:T(8,128)S(1)} %broadcast_select_fusion.4), channel_id=1, source_target_pairs={{0,32},{32,64},{64,96},{96,128},{128,160},{160,192},{192,224},{224... | collective-permute-start | bytes 24584 | tf_op jit(solution)/shard_map/while/body/eval_jaxpr/ppermute | solution.py:25
  202.8 5.8 %collective-permute-start.1 = (f32[1,16,128]{2,1,0:T(8,128)S(1)}, f32[1,16,128]{2,1,0:T(8,128)S(1)}, u32[]{:S(2)}, u32[]{:S(2)}) collective-permute-start(f32[1,16,128]{2,1,0:T(8,128)S(1)} %broadcast_select_fusion.5), channel_id=1, source_target_pairs={{1,0},{2,1},{3,2},{4,3},{5,4},{6,5},{7,6},{8,7},{9,8},{10,9},{11,1... | collective-permute-start | bytes 24584 | tf_op jit(solution)/shard_map/while/body/eval_jaxpr/ppermute | solution.py:17
  204.7 7.7 %collective-permute-start.2 = (f32[1,16,128]{2,1,0:T(8,128)S(1)}, f32[1,16,128]{2,1,0:T(8,128)S(1)}, u32[]{:S(2)}, u32[]{:S(2)}) collective-permute-start(f32[1,16,128]{2,1,0:T(8,128)S(1)} %broadcast_select_fusion.5), channel_id=1, source_target_pairs={{0,1},{1,2},{2,3},{3,4},{4,5},{5,6},{6,7},{7,8},{8,9},{9,10},{10,1... | collective-permute-start | bytes 24584 | tf_op jit(solution)/shard_map/while/body/eval_jaxpr/ppermute | solution.py:16
  212.6 8.6 %collective-permute-start = (f32[1,16,128]{2,1,0:T(8,128)S(1)}, f32[1,16,128]{2,1,0:T(8,128)S(1)}, u32[]{:S(2)}, u32[]{:S(2)}) collective-permute-start(f32[1,16,128]{2,1,0:T(8,128)S(1)} %broadcast_select_fusion.4), channel_id=1, source_target_pairs={{0,32},{32,64},{64,96},{96,128},{128,160},{160,192},{192,224},{224... | collective-permute-start | bytes 24584 | tf_op jit(solution)/shard_map/while/body/eval_jaxpr/ppermute | solution.py:25
  221.2 5.8 %collective-permute-start.1 = (f32[1,16,128]{2,1,0:T(8,128)S(1)}, f32[1,16,128]{2,1,0:T(8,128)S(1)}, u32[]{:S(2)}, u32[]{:S(2)}) collective-permute-start(f32[1,16,128]{2,1,0:T(8,128)S(1)} %broadcast_select_fusion.5), channel_id=1, source_target_pairs={{1,0},{2,1},{3,2},{4,3},{5,4},{6,5},{7,6},{8,7},{9,8},{10,9},{11,1... | collective-permute-start | bytes 24584 | tf_op jit(solution)/shard_map/while/body/eval_jaxpr/ppermute | solution.py:17
  223.1 7.7 %collective-permute-start.2 = (f32[1,16,128]{2,1,0:T(8,128)S(1)}, f32[1,16,128]{2,1,0:T(8,128)S(1)}, u32[]{:S(2)}, u32[]{:S(2)}) collective-permute-start(f32[1,16,128]{2,1,0:T(8,128)S(1)} %broadcast_select_fusion.5), channel_id=1, source_target_pairs={{0,1},{1,2},{2,3},{3,4},{4,5},{5,6},{6,7},{7,8},{8,9},{9,10},{10,1... | collective-permute-start | bytes 24584 | tf_op jit(solution)/shard_map/while/body/eval_jaxpr/ppermute | solution.py:16
  231.0 8.6 %collective-permute-start = (f32[1,16,128]{2,1,0:T(8,128)S(1)}, f32[1,16,128]{2,1,0:T(8,128)S(1)}, u32[]{:S(2)}, u32[]{:S(2)}) collective-permute-start(f32[1,16,128]{2,1,0:T(8,128)S(1)} %broadcast_select_fusion.4), channel_id=1, source_target_pairs={{0,32},{32,64},{64,96},{96,128},{128,160},{160,192},{192,224},{224... | collective-permute-start | bytes 24584 | tf_op jit(solution)/shard_map/while/body/eval_jaxpr/ppermute | solution.py:25
  241.5 7.7 %collective-permute-start.2 = (f32[1,16,128]{2,1,0:T(8,128)S(1)}, f32[1,16,128]{2,1,0:T(8,128)S(1)}, u32[]{:S(2)}, u32[]{:S(2)}) collective-permute-start(f32[1,16,128]{2,1,0:T(8,128)S(1)} %broadcast_select_fusion.5), channel_id=1, source_target_pairs={{0,1},{1,2},{2,3},{3,4},{4,5},{5,6},{6,7},{7,8},{8,9},{9,10},{10,1... | collective-permute-start | bytes 24584 | tf_op jit(solution)/shard_map/while/body/eval_jaxpr/ppermute | solution.py:16
  249.3 8.6 %collective-permute-start = (f32[1,16,128]{2,1,0:T(8,128)S(1)}, f32[1,16,128]{2,1,0:T(8,128)S(1)}, u32[]{:S(2)}, u32[]{:S(2)}) collective-permute-start(f32[1,16,128]{2,1,0:T(8,128)S(1)} %broadcast_select_fusion.4), channel_id=1, source_target_pairs={{0,32},{32,64},{64,96},{96,128},{128,160},{160,192},{192,224},{224... | collective-permute-start | bytes 24584 | tf_op jit(solution)/shard_map/while/body/eval_jaxpr/ppermute | solution.py:25
  257.9 5.8 %collective-permute-start.1 = (f32[1,16,128]{2,1,0:T(8,128)S(1)}, f32[1,16,128]{2,1,0:T(8,128)S(1)}, u32[]{:S(2)}, u32[]{:S(2)}) collective-permute-start(f32[1,16,128]{2,1,0:T(8,128)S(1)} %broadcast_select_fusion.5), channel_id=1, source_target_pairs={{1,0},{2,1},{3,2},{4,3},{5,4},{6,5},{7,6},{8,7},{9,8},{10,9},{11,1... | collective-permute-start | bytes 24584 | tf_op jit(solution)/shard_map/while/body/eval_jaxpr/ppermute | solution.py:17
  259.8 7.7 %collective-permute-start.2 = (f32[1,16,128]{2,1,0:T(8,128)S(1)}, f32[1,16,128]{2,1,0:T(8,128)S(1)}, u32[]{:S(2)}, u32[]{:S(2)}) collective-permute-start(f32[1,16,128]{2,1,0:T(8,128)S(1)} %broadcast_select_fusion.5), channel_id=1, source_target_pairs={{0,1},{1,2},{2,3},{3,4},{4,5},{5,6},{6,7},{7,8},{8,9},{9,10},{10,1... | collective-permute-start | bytes 24584 | tf_op jit(solution)/shard_map/while/body/eval_jaxpr/ppermute | solution.py:16
  267.7 8.6 %collective-permute-start = (f32[1,16,128]{2,1,0:T(8,128)S(1)}, f32[1,16,128]{2,1,0:T(8,128)S(1)}, u32[]{:S(2)}, u32[]{:S(2)}) collective-permute-start(f32[1,16,128]{2,1,0:T(8,128)S(1)} %broadcast_select_fusion.4), channel_id=1, source_target_pairs={{0,32},{32,64},{64,96},{96,128},{128,160},{160,192},{192,224},{224... | collective-permute-start | bytes 24584 | tf_op jit(solution)/shard_map/while/body/eval_jaxpr/ppermute | solution.py:25
  276.3 5.8 %collective-permute-start.1 = (f32[1,16,128]{2,1,0:T(8,128)S(1)}, f32[1,16,128]{2,1,0:T(8,128)S(1)}, u32[]{:S(2)}, u32[]{:S(2)}) collective-permute-start(f32[1,16,128]{2,1,0:T(8,128)S(1)} %broadcast_select_fusion.5), channel_id=1, source_target_pairs={{1,0},{2,1},{3,2},{4,3},{5,4},{6,5},{7,6},{8,7},{9,8},{10,9},{11,1... | collective-permute-start | bytes 24584 | tf_op jit(solution)/shard_map/while/body/eval_jaxpr/ppermute | solution.py:17
  278.2 7.7 %collective-permute-start.2 = (f32[1,16,128]{2,1,0:T(8,128)S(1)}, f32[1,16,128]{2,1,0:T(8,128)S(1)}, u32[]{:S(2)}, u32[]{:S(2)}) collective-permute-start(f32[1,16,128]{2,1,0:T(8,128)S(1)} %broadcast_select_fusion.5), channel_id=1, source_target_pairs={{0,1},{1,2},{2,3},{3,4},{4,5},{5,6},{6,7},{7,8},{8,9},{9,10},{10,1... | collective-permute-start | bytes 24584 | tf_op jit(solution)/shard_map/while/body/eval_jaxpr/ppermute | solution.py:16
  286.1 8.6 %collective-permute-start = (f32[1,16,128]{2,1,0:T(8,128)S(1)}, f32[1,16,128]{2,1,0:T(8,128)S(1)}, u32[]{:S(2)}, u32[]{:S(2)}) collective-permute-start(f32[1,16,128]{2,1,0:T(8,128)S(1)} %broadcast_select_fusion.4), channel_id=1, source_target_pairs={{0,32},{32,64},{64,96},{96,128},{128,160},{160,192},{192,224},{224... | collective-permute-start | bytes 24584 | tf_op jit(solution)/shard_map/while/body/eval_jaxpr/ppermute | solution.py:25
  294.7 5.8 %collective-permute-start.1 = (f32[1,16,128]{2,1,0:T(8,128)S(1)}, f32[1,16,128]{2,1,0:T(8,128)S(1)}, u32[]{:S(2)}, u32[]{:S(2)}) collective-permute-start(f32[1,16,128]{2,1,0:T(8,128)S(1)} %broadcast_select_fusion.5), channel_id=1, source_target_pairs={{1,0},{2,1},{3,2},{4,3},{5,4},{6,5},{7,6},{8,7},{9,8},{10,9},{11,1... | collective-permute-start | bytes 24584 | tf_op jit(solution)/shard_map/while/body/eval_jaxpr/ppermute | solution.py:17
  296.6 7.7 %collective-permute-start.2 = (f32[1,16,128]{2,1,0:T(8,128)S(1)}, f32[1,16,128]{2,1,0:T(8,128)S(1)}, u32[]{:S(2)}, u32[]{:S(2)}) collective-permute-start(f32[1,16,128]{2,1,0:T(8,128)S(1)} %broadcast_select_fusion.5), channel_id=1, source_target_pairs={{0,1},{1,2},{2,3},{3,4},{4,5},{5,6},{6,7},{7,8},{8,9},{9,10},{10,1... | collective-permute-start | bytes 24584 | tf_op jit(solution)/shard_map/while/body/eval_jaxpr/ppermute | solution.py:16
  304.4 8.6 %collective-permute-start = (f32[1,16,128]{2,1,0:T(8,128)S(1)}, f32[1,16,128]{2,1,0:T(8,128)S(1)}, u32[]{:S(2)}, u32[]{:S(2)}) collective-permute-start(f32[1,16,128]{2,1,0:T(8,128)S(1)} %broadcast_select_fusion.4), channel_id=1, source_target_pairs={{0,32},{32,64},{64,96},{96,128},{128,160},{160,192},{192,224},{224... | collective-permute-start | bytes 24584 | tf_op jit(solution)/shard_map/while/body/eval_jaxpr/ppermute | solution.py:25
  314.9 7.7 %collective-permute-start.2 = (f32[1,16,128]{2,1,0:T(8,128)S(1)}, f32[1,16,128]{2,1,0:T(8,128)S(1)}, u32[]{:S(2)}, u32[]{:S(2)}) collective-permute-start(f32[1,16,128]{2,1,0:T(8,128)S(1)} %broadcast_select_fusion.5), channel_id=1, source_target_pairs={{0,1},{1,2},{2,3},{3,4},{4,5},{5,6},{6,7},{7,8},{8,9},{9,10},{10,1... | collective-permute-start | bytes 24584 | tf_op jit(solution)/shard_map/while/body/eval_jaxpr/ppermute | solution.py:16
  322.8 8.6 %collective-permute-start = (f32[1,16,128]{2,1,0:T(8,128)S(1)}, f32[1,16,128]{2,1,0:T(8,128)S(1)}, u32[]{:S(2)}, u32[]{:S(2)}) collective-permute-start(f32[1,16,128]{2,1,0:T(8,128)S(1)} %broadcast_select_fusion.4), channel_id=1, source_target_pairs={{0,32},{32,64},{64,96},{96,128},{128,160},{160,192},{192,224},{224... | collective-permute-start | bytes 24584 | tf_op jit(solution)/shard_map/while/body/eval_jaxpr/ppermute | solution.py:25
  333.3 7.7 %collective-permute-start.2 = (f32[1,16,128]{2,1,0:T(8,128)S(1)}, f32[1,16,128]{2,1,0:T(8,128)S(1)}, u32[]{:S(2)}, u32[]{:S(2)}) collective-permute-start(f32[1,16,128]{2,1,0:T(8,128)S(1)} %broadcast_select_fusion.5), channel_id=1, source_target_pairs={{0,1},{1,2},{2,3},{3,4},{4,5},{5,6},{6,7},{7,8},{8,9},{9,10},{10,1... | collective-permute-start | bytes 24584 | tf_op jit(solution)/shard_map/while/body/eval_jaxpr/ppermute | solution.py:16
  (9 other events, 65.4 us)
where the time goes:
time: 344 us; the launch traced here: 342 us
  waiting for transfers between devices  170 us (49%)
  starting transfers between devices  147 us (43%)
  local copies, waits for them, and re-layouts  14.1 us (4%)
  other arithmetic  9.84 us (3%)
    ppermute x16, waiting for transfers between devices, passed_along(): return lax.ppermute(shard, axis, pairs)  106 us
    ppermute x19, starting transfers between devices, with_halo(): before = lax.ppermute(last, axis, up)  67.9 us
    ppermute x19, waiting for transfers between devices, with_halo(): before = lax.ppermute(last, axis, up)  63.5 us
    ppermute x19, starting transfers between devices, with_halo(): after = lax.ppermute(leading, axis, down)  48 us
    ppermute x16, starting transfers between devices, passed_along(): return lax.ppermute(shard, axis, pairs)  30.7 us
    reduce_sum x4, local copies, waits for them, and re-layouts, restrict(): return jnp.mean(shaped, axis=(-5, -3, -1))  13.9 us
  transfers between devices with their start and end apart: 54, of which 33 were waited for; matrix products, arithmetic and copies ran while one was open for 4% of the time, Pallas kernels for 0%

commit v1 on v0

v1 whole, which is shorter than its diff:
```python
import jax
import jax.numpy as jnp
from jax import lax
from jax.experimental import pallas as pl
from jax.experimental.pallas import tpu as pltpu
from jax.sharding import PartitionSpec as P

MESH = pl.DeviceIdType.MESH
REACH = 7
GREET = 8
NEAR = (1, 2, 3)
MID = 4
FAR = 8


def seven(diffusivity, vx, vy, vz, spread, first, last):
    ak = spread * diffusivity
    hx, hy, hz = 0.5 * vx, 0.5 * vy, 0.5 * vz
    rows = lax.broadcasted_iota(jnp.int32, ak.shape, ak.ndim - 2)
    cols = lax.broadcasted_iota(jnp.int32, ak.shape, ak.ndim - 1)
    zero = jnp.zeros_like(ak)
    return (
        1.0 - 6.0 * ak,
        (ak + hx) * first,
        (ak - hx) * last,
        jnp.where(rows == 0, zero, ak + hy),
        jnp.where(rows == ak.shape[-2] - 1, zero, ak - hy),
        jnp.where(cols == 0, zero, ak + hz),
        jnp.where(cols == ak.shape[-1] - 1, zero, ak - hz),
    )


def inplane(factors, f):
    c0, _, _, ym, yp, zm, zp = factors
    a, b = f.ndim - 2, f.ndim - 1
    return (
        c0 * f
        + (ym * pltpu.roll(f, 1, a) + yp * pltpu.roll(f, f.shape[a] - 1, a))
        + (zm * pltpu.roll(f, 1, b) + zp * pltpu.roll(f, f.shape[b] - 1, b))
    )


def restrict(work, two):
    rows = two.shape[1]
    both = two[0] + two[1]
    lanes = lax.broadcasted_iota(jnp.int32, (rows // 2, 128), 1)
    place = lax.rem(2 * lanes, 128)
    sides = []
    for h in range(2):
        work[h] = both[:, 128 * h : 128 * (h + 1)]
        half = work[h, pl.ds(0, rows // 2, 2), :] + work[h, pl.ds(1, rows // 2, 2), :]
        half = half + pltpu.roll(half, 127, 1)
        sides.append(jnp.take_along_axis(half, place, axis=1))
    return 0.125 * jnp.where(lanes < 64, sides[0], sides[1])


def kernel(
    nt, ns, init, vel, dif, fine_out, delta_out,
    f_ref, v_ref, k_ref, work, left0, right0, left1, right1, mid1,
    start_own, start_left, start_right, coef, kap,
    r_ref, u_ref, w_ref, near1, near2, near3, mid, far,
    load_sem, halo_send, halo_recv, coef_send, coef_recv, hop_send, hop_recv, ready,
):
    t, s = lax.axis_index("tm"), lax.axis_index("space")
    core = lax.rem(t, 2)
    sibling = t + 1 - 2 * core
    near = (near1, near2, near3)

    def at(ds):
        return lax.rem(s + (ds + ns), ns)

    for j, slot in zip(NEAR, near):

        @pl.when(t < j)
        def _():
            slot[...] = jnp.zeros_like(slot)

    barrier = pltpu.get_barrier_semaphore()
    for k in range(1, GREET + 1):
        for ds in (k, -k):
            pl.semaphore_signal(barrier, inc=1, device_id=(t, at(ds)), device_id_type=MESH)
    pl.semaphore_signal(barrier, inc=1, device_id=(sibling, s), device_id_type=MESH)
    for j in NEAR + (MID, FAR):

        @pl.when(t + j < nt)
        def _():
            pl.semaphore_signal(barrier, inc=1, device_id=(t + j, s), device_id_type=MESH)

    loads = [
        pltpu.make_async_copy(a, b, load_sem.at[i])
        for i, (a, b) in enumerate(((init.at[0], f_ref), (vel, v_ref), (dif, k_ref)))
    ]
    for copy in loads:
        copy.start()
    senders = sum(jnp.where(t >= j, 1, 0) for j in NEAR + (MID, FAR))
    pl.semaphore_wait(barrier, 2 * GREET + 1 + senders)

    def remote(src, dst, send, recv, tt, ds):
        return pltpu.make_async_remote_copy(
            src_ref=src, dst_ref=dst, send_sem=send, recv_sem=recv, device_id=(tt, at(ds)), device_id_type=MESH
        )

    halo0 = [
        remote(init.at[0, 0], right0, halo_send.at[0], halo_recv.at[0], t, -1),
        remote(init.at[0, 1], left0, halo_send.at[1], halo_recv.at[1], t, 1),
    ]
    for copy in halo0:
        copy.start()

    for i, j in enumerate(NEAR + (MID, FAR)):

        @pl.when(t >= j)
        def _():
            pl.semaphore_signal(ready.at[i], inc=1, device_id=(t - j, s), device_id_type=MESH)

    loads[0].wait()
    start = restrict(work, f_ref)
    start_own[...] = start
    halo_c = [
        remote(start_own, start_right, halo_send.at[2], halo_recv.at[2], t, -1),
        remote(start_own, start_left, halo_send.at[3], halo_recv.at[3], t, 1),
    ]
    for copy in halo_c:
        copy.start()

    loads[1].wait()
    loads[2].wait()
    coarse = [restrict(work, v_ref[0]), restrict(work, v_ref[1]), restrict(work, v_ref[2]), restrict(work, k_ref)]
    for i in range(2):
        coef[core, REACH, i] = jnp.where(core == 0, coarse[i], coarse[2 + i])
    coef_out = []
    for k in range(1, REACH + 1):
        for ds in (k, -k):
            copy = remote(coef.at[core, REACH], coef.at[core, REACH - ds], coef_send.at[0], coef_recv.at[0], t, ds)
            copy.start()
            coef_out.append(copy)

    one = jnp.float32(1.0)
    first = jnp.where(s == 0, 0.0, one)
    last = jnp.where(s == ns - 1, 0.0, one)
    fine0 = seven(k_ref[0], v_ref[0, 0], v_ref[1, 0], v_ref[2, 0], 1.0, first, one)
    fine1 = seven(k_ref[1], v_ref[0, 1], v_ref[1, 1], v_ref[2, 1], 1.0, one, last)

    def partial(a, b):
        return inplane(fine0, a) + fine0[2] * b, inplane(fine1, b) + fine1[1] * a

    pa, pb = partial(f_ref[0], f_ref[1])
    for copy in halo0:
        copy.wait_recv()
    mid1[0] = pa + fine0[1] * left0[...]
    mid1[1] = pb + fine1[2] * right0[...]
    halo1 = [
        remote(mid1.at[0], right1, halo_send.at[4], halo_recv.at[4], t, -1),
        remote(mid1.at[1], left1, halo_send.at[5], halo_recv.at[5], t, 1),
    ]
    for copy in halo1:
        copy.start()

    pa, pb = partial(mid1[0], mid1[1])
    own = seven(coarse[3], coarse[0], coarse[1], coarse[2], 0.5, first, last)
    for copy in halo_c:
        copy.wait_recv()
    stepped = inplane(own, start) + (own[1] * start_left[...] + own[2] * start_right[...])
    for copy in halo1:
        copy.wait_recv()
    fine_out[0] = pa + fine0[1] * left1[...]
    fine_out[1] = pb + fine1[2] * right1[...]
    end = restrict(work, fine_out)
    r_ref[...] = end - jnp.where(t == 0, 0.0, one) * stepped

    def hop(number, dt, src, slot):
        @pl.when(t + dt < nt)
        def _():
            pl.semaphore_wait(ready.at[number], 1)
            for ds in range(-dt, dt + 1):
                remote(src, slot.at[dt - ds], hop_send.at[number], hop_recv.at[number], t + dt, ds).start()

    def arrived(number, dt, slot):
        @pl.when(t >= dt)
        def _():
            pltpu.make_async_copy(slot, slot, hop_recv.at[number]).wait()

    def sent(number, dt, slot):
        @pl.when(t + dt < nt)
        def _():
            pltpu.make_async_copy(slot, slot, hop_send.at[number]).wait()

    for i, j in enumerate(NEAR):
        hop(i, j, r_ref, near[i])

    some = coef.at[0, 0 : 2 * REACH]
    pltpu.make_async_copy(some, some, coef_recv.at[0]).wait()
    share = remote(coef.at[core], coef.at[core], coef_send.at[1], coef_recv.at[1], sibling, 0)
    share.start()
    share.wait_recv()
    for p in range(-REACH, REACH + 1):
        i = p + REACH
        position = at(p)
        factors = seven(
            coef[1, i, 1], coef[0, i, 0], coef[0, i, 1], coef[1, i, 0], 0.5,
            jnp.where(position == 0, 0.0, one), jnp.where(position == ns - 1, 0.0, one),
        )
        for n in range(7):
            kap[n, i] = factors[n]

    def coarse_step(v):
        w = (v.shape[0] - 3) // 2
        factors = [kap[n, REACH - w : REACH + w + 1] for n in range(7)]
        return inplane(factors, v[1:-1]) + (factors[1] * v[:-2] + factors[2] * v[2:])

    for i, j in enumerate(NEAR):
        arrived(i, j, near[i])
    v = near3[...]
    v = coarse_step(v) + near2[...]
    v = coarse_step(v) + near1[...]
    u_ref[...] = coarse_step(v)[0] + r_ref[...]

    hop(3, MID, u_ref, mid)
    arrived(3, MID, mid)

    @pl.when(t >= MID)
    def _():
        v = mid[...]
        for _ in range(MID):
            v = coarse_step(v)
        w_ref[...] = v[0] + u_ref[...]

    @pl.when(t < MID)
    def _():
        w_ref[...] = u_ref[...]

    hop(4, FAR, w_ref, far)
    arrived(4, FAR, far)

    def finish(c):
        d = c - end
        lanes = lax.broadcasted_iota(jnp.int32, d.shape, 1)
        for h in range(2):
            wide = jnp.take_along_axis(d, lanes // 2 + 64 * h, axis=1)
            for i in range(2):
                work[h, pl.ds(i, d.shape[0], 2), :] = wide
            delta_out[:, 128 * h : 128 * (h + 1)] = work[h]

    @pl.when(t >= FAR)
    def _():
        v = far[...]
        for _ in range(FAR):
            v = coarse_step(v)
        finish(v[0] + w_ref[...])

    @pl.when(t < FAR)
    def _():
        finish(w_ref[...])

    for copy in halo0 + halo_c + halo1:
        copy.wait_send()
    pltpu.make_async_copy(some, some, coef_send.at[0]).wait()
    share.wait_send()
    for i, j in enumerate(NEAR):
        sent(i, j, near[i])
    sent(3, MID, mid)
    sent(4, FAR, far)


def solution(mesh):
    nt, ns = mesh.shape["tm"], mesh.shape["space"]

    def shards(initial_states, velocity, diffusivity):
        _, planes, cy, cz = initial_states.shape
        fine = (planes, cy, cz)
        plane, small = (cy, cz), (cy // 2, cz // 2)

        def vmem(*shape):
            return pltpu.VMEM(shape, jnp.float32)

        dma = pltpu.SemaphoreType.DMA
        ended, delta = pl.pallas_call(
            lambda *refs: kernel(nt, ns, *refs),
            out_shape=(jax.ShapeDtypeStruct(fine, jnp.float32), jax.ShapeDtypeStruct(plane, jnp.float32)),
            in_specs=[pl.BlockSpec(memory_space=pl.ANY)] * 3,
            out_specs=(pl.BlockSpec(memory_space=pltpu.VMEM),) * 2,
            scratch_shapes=[
                vmem(*fine), vmem(3, *fine), vmem(*fine), vmem(2, cy, cz // 2),
                vmem(*plane), vmem(*plane), vmem(*plane), vmem(*plane), vmem(*fine),
                vmem(*small), vmem(*small), vmem(*small),
                vmem(2, 2 * REACH + 1, 2, *small), vmem(7, 2 * REACH + 1, *small),
                vmem(*small), vmem(*small), vmem(*small),
                *(vmem(2 * j + 1, *small) for j in NEAR), vmem(2 * MID + 1, *small), vmem(2 * FAR + 1, *small),
                dma((3,)), dma((6,)), dma((6,)), dma((2,)), dma((2,)), dma((5,)), dma((5,)),
                pltpu.SemaphoreType.REGULAR((5,)),
            ],
            compiler_params=pltpu.CompilerParams(collective_id=0, has_side_effects=True),
        )(initial_states, velocity, diffusivity)
        return (ended + delta[None])[None]

    in_specs = (P("tm", "space", None, None), P(None, "space", None, None), P("space", None, None))
    out_specs = P("tm", "space", None, None)
    return jax.shard_map(shards, mesh=mesh, in_specs=in_specs, out_specs=out_specs, check_vma=False)
```

time: 344 us -> 42.2 us (0.12)
  the two profiles are of different devices: /device:TPU:388 before, /device:TPU:31 now
where the time goes in v1:
time: 42.2 us; the launch traced here: 42 us
  Pallas kernels  40.5 us (96%)
  other arithmetic  1.48 us (4%)
    pallas_call x1, Pallas kernels, shards(): pl.pallas_call(lambda *refs: kernel(nt, ns, *refs), out_shape=(jax.ShapeD...  40.5 us
    broadcast_in_dim x1, other arithmetic, shards(): return (ended + delta[None])[None]  1.48 us

profile of v1, /device:TPU:31, one launch (start us, length us, event | category | flops | bytes accessed | tf_op | source)
XLA Modules:
  0.0 42.0 jit_solution(6904733447790971732)
XLA Ops:
  0.0 40.5 %shard_map.37 = (f32[2,32,256]{2,1,0:T(8,128)}, f32[32,256]{1,0:T(8,128)}) custom-call(f32[1,2,32,256]{3,2,1,0:T(8,128)} %refs_0_.1, f32[3,2,32,256]{3,2,1,0:T(8,128)} %refs_1_.1, f32[2,32,256]{2,1,0:T(8,128)} %refs_2_.1), custom_call_target="tpu_custom_call" | custom-call | tf_op jit(solution)/shard_map/pallas_call | solution.py:277
  40.5 1.5 %add_bitcast_fusion = f32[1,2,32,256]{3,2,1,0:T(8,128)} fusion(f32[2,32,256]{2,1,0:T(8,128)} %get-tuple-element.7, f32[32,256]{1,0:T(8,128)} %get-tuple-element.8), kind=kLoop, calls=%fused_computation | loop fusion | flops 16384 | bytes 163840 | tf_op jit(solution)/shard_map/broadcast_in_dim | solution.py:294

commit v2 on v1

--- a/solution.py
+++ b/solution.py
@@ -1,3 +1,5 @@
+import functools
+
 import jax
 import jax.numpy as jnp
 from jax import lax
@@ -13,7 +15,7 @@
 FAR = 8
 
 
-def seven(diffusivity, vx, vy, vz, spread, first, last):
+def seven(diffusivity, vx, vy, vz, spread):
     ak = spread * diffusivity
     hx, hy, hz = 0.5 * vx, 0.5 * vy, 0.5 * vz
     rows = lax.broadcasted_iota(jnp.int32, ak.shape, ak.ndim - 2)
@@ -21,8 +23,8 @@
     zero = jnp.zeros_like(ak)
     return (
         1.0 - 6.0 * ak,
-        (ak + hx) * first,
-        (ak - hx) * last,
+        ak + hx,
+        ak - hx,
         jnp.where(rows == 0, zero, ak + hy),
         jnp.where(rows == ak.shape[-2] - 1, zero, ak - hy),
         jnp.where(cols == 0, zero, ak + hz),
@@ -66,8 +68,11 @@
     sibling = t + 1 - 2 * core
     near = (near1, near2, near3)
 
-    def at(ds):
-        return lax.rem(s + (ds + ns), ns)
+    def inside(ds):
+        return s + ds < ns if ds > 0 else s + ds >= 0
+
+    def outward(width):
+        return [ds for k in range(width, 0, -1) for ds in (k, -k)]
 
     for j, slot in zip(NEAR, near):
 
@@ -75,10 +80,28 @@
         def _():
             slot[...] = jnp.zeros_like(slot)
 
+    @pl.when((s < FAR) | (s >= ns - FAR))
+    def _():
+        for slot in (near1, near2, near3, mid, far, coef):
+            slot[...] = jnp.zeros_like(slot)
+
+    @pl.when(s == 0)
+    def _():
+        for slot in (left0, left1, start_left):
+            slot[...] = jnp.zeros_like(slot)
+
+    @pl.when(s == ns - 1)
+    def _():
+        for slot in (right0, right1, start_right):
+            slot[...] = jnp.zeros_like(slot)
+
     barrier = pltpu.get_barrier_semaphore()
-    for k in range(1, GREET + 1):
-        for ds in (k, -k):
-            pl.semaphore_signal(barrier, inc=1, device_id=(t, at(ds)), device_id_type=MESH)
+    for ds in reversed(outward(GREET)):
+
+        @pl.when(inside(ds))
+        def _():
+            pl.semaphore_signal(barrier, inc=1, device_id=(t, s + ds), device_id_type=MESH)
+
     pl.semaphore_signal(barrier, inc=1, device_id=(sibling, s), device_id_type=MESH)
     for j in NEAR + (MID, FAR):
 
@@ -93,19 +116,41 @@
     for copy in loads:
         copy.start()
     senders = sum(jnp.where(t >= j, 1, 0) for j in NEAR + (MID, FAR))
-    pl.semaphore_wait(barrier, 2 * GREET + 1 + senders)
+    beside = jnp.minimum(s, GREET) + jnp.minimum(ns - 1 - s, GREET)
+    pl.semaphore_wait(barrier, beside + 1 + senders)
 
     def remote(src, dst, send, recv, tt, ds):
         return pltpu.make_async_remote_copy(
-            src_ref=src, dst_ref=dst, send_sem=send, recv_sem=recv, device_id=(tt, at(ds)), device_id_type=MESH
+            src_ref=src, dst_ref=dst, send_sem=send, recv_sem=recv, device_id=(tt, s + ds), device_id_type=MESH
         )
 
+    def beside_do(pair, what):
+        down, up = pair
+
+        @pl.when(s > 0)
+        def _():
+            if what == "start":
+                down.start()
+            elif what == "recv":
+                up.wait_recv()
+            else:
+                down.wait_send()
+
+        @pl.when(s < ns - 1)
+        def _():
+            if what == "start":
+                up.start()
+            elif what == "recv":
+                down.wait_recv()
+            else:
+                up.wait_send()
+
+    loads[0].wait()
     halo0 = [
-        remote(init.at[0, 0], right0, halo_send.at[0], halo_recv.at[0], t, -1),
-        remote(init.at[0, 1], left0, halo_send.at[1], halo_recv.at[1], t, 1),
+        remote(f_ref.at[0], right0, halo_send.at[0], halo_recv.at[0], t, -1),
+        remote(f_ref.at[1], left0, halo_send.at[1], halo_recv.at[1], t, 1),
     ]
-    for copy in halo0:
-        copy.start()
+    beside_do(halo0, "start")
 
     for i, j in enumerate(NEAR + (MID, FAR)):
 
@@ -113,93 +158,110 @@
         def _():
             pl.semaphore_signal(ready.at[i], inc=1, device_id=(t - j, s), device_id_type=MESH)
 
-    loads[0].wait()
     start = restrict(work, f_ref)
     start_own[...] = start
     halo_c = [
         remote(start_own, start_right, halo_send.at[2], halo_recv.at[2], t, -1),
         remote(start_own, start_left, halo_send.at[3], halo_recv.at[3], t, 1),
     ]
-    for copy in halo_c:
-        copy.start()
+    beside_do(halo_c, "start")
 
     loads[1].wait()
     loads[2].wait()
     coarse = [restrict(work, v_ref[0]), restrict(work, v_ref[1]), restrict(work, v_ref[2]), restrict(work, k_ref)]
     for i in range(2):
         coef[core, REACH, i] = jnp.where(core == 0, coarse[i], coarse[2 + i])
-    coef_out = []
-    for k in range(1, REACH + 1):
-        for ds in (k, -k):
-            copy = remote(coef.at[core, REACH], coef.at[core, REACH - ds], coef_send.at[0], coef_recv.at[0], t, ds)
-            copy.start()
-            coef_out.append(copy)
+    for ds in reversed(outward(REACH)):
+
+        @pl.when(inside(ds))
+        def _():
+            i = REACH - ds
+            remote(coef.at[core, REACH], coef.at[core, i], coef_send.at[i], coef_recv.at[i], t, ds).start()
+
 
     one = jnp.float32(1.0)
-    first = jnp.where(s == 0, 0.0, one)
-    last = jnp.where(s == ns - 1, 0.0, one)
-    fine0 = seven(k_ref[0], v_ref[0, 0], v_ref[1, 0], v_ref[2, 0], 1.0, first, one)
-    fine1 = seven(k_ref[1], v_ref[0, 1], v_ref[1, 1], v_ref[2, 1], 1.0, one, last)
+    fine0 = seven(k_ref[0], v_ref[0, 0], v_ref[1, 0], v_ref[2, 0], 1.0)
+    fine1 = seven(k_ref[1], v_ref[0, 1], v_ref[1, 1], v_ref[2, 1], 1.0)
 
     def partial(a, b):
         return inplane(fine0, a) + fine0[2] * b, inplane(fine1, b) + fine1[1] * a
 
     pa, pb = partial(f_ref[0], f_ref[1])
-    for copy in halo0:
-        copy.wait_recv()
+    beside_do(halo0, "recv")
     mid1[0] = pa + fine0[1] * left0[...]
     mid1[1] = pb + fine1[2] * right0[...]
     halo1 = [
         remote(mid1.at[0], right1, halo_send.at[4], halo_recv.at[4], t, -1),
         remote(mid1.at[1], left1, halo_send.at[5], halo_recv.at[5], t, 1),
     ]
-    for copy in halo1:
-        copy.start()
+    beside_do(halo1, "start")
 
     pa, pb = partial(mid1[0], mid1[1])
-    own = seven(coarse[3], coarse[0], coarse[1], coarse[2], 0.5, first, last)
-    for copy in halo_c:
-        copy.wait_recv()
+    own = seven(coarse[3], coarse[0], coarse[1], coarse[2], 0.5)
+    beside_do(halo_c, "recv")
     stepped = inplane(own, start) + (own[1] * start_left[...] + own[2] * start_right[...])
-    for copy in halo1:
-        copy.wait_recv()
+    beside_do(halo1, "recv")
     fine_out[0] = pa + fine0[1] * left1[...]
     fine_out[1] = pb + fine1[2] * right1[...]
     end = restrict(work, fine_out)
     r_ref[...] = end - jnp.where(t == 0, 0.0, one) * stepped
 
+    def each(width, slot, sem, mirrored):
+        low, high = jnp.minimum(s, width), jnp.minimum(ns - 1 - s, width)
+        if mirrored:
+            low, high = high, low
+
+        def one_of(i, _):
+            pltpu.make_async_copy(slot(i), slot(i), sem(i)).wait()
+            return 0
+
+        lax.fori_loop(width - low, width + high + 1, one_of, 0)
+
     def hop(number, dt, src, slot):
         @pl.when(t + dt < nt)
         def _():
             pl.semaphore_wait(ready.at[number], 1)
-            for ds in range(-dt, dt + 1):
-                remote(src, slot.at[dt - ds], hop_send.at[number], hop_recv.at[number], t + dt, ds).start()
+
+            def send(ds):
+                i = dt - ds
+                remote(src, slot.at[i], hop_send.at[number, i], hop_recv.at[number, i], t + dt, ds).start()
+
+            for ds in outward(dt):
+                pl.when(inside(ds))(functools.partial(send, ds))
+            send(0)
 
     def arrived(number, dt, slot):
         @pl.when(t >= dt)
         def _():
-            pltpu.make_async_copy(slot, slot, hop_recv.at[number]).wait()
+            each(dt, lambda i: slot.at[i], lambda i: hop_recv.at[number, i], False)
 
     def sent(number, dt, slot):
         @pl.when(t + dt < nt)
         def _():
-            pltpu.make_async_copy(slot, slot, hop_send.at[number]).wait()
+            each(dt, lambda i: slot.at[i], lambda i: hop_send.at[number, i], True)
 
     for i, j in enumerate(NEAR):
         hop(i, j, r_ref, near[i])
 
-    some = coef.at[0, 0 : 2 * REACH]
-    pltpu.make_async_copy(some, some, coef_recv.at[0]).wait()
-    share = remote(coef.at[core], coef.at[core], coef_send.at[1], coef_recv.at[1], sibling, 0)
+    def around(sem, mirrored):
+        low, high = jnp.minimum(s, REACH), jnp.minimum(ns - 1 - s, REACH)
+        if mirrored:
+            low, high = high, low
+
+        def one_of(i, _):
+            pltpu.make_async_copy(coef.at[core, i], coef.at[core, i], sem.at[i]).wait()
+            return 0
+
+        lax.fori_loop(REACH - low, REACH, one_of, 0)
+        lax.fori_loop(REACH + 1, REACH + high + 1, one_of, 0)
+
+    around(coef_recv, False)
+    share = remote(coef.at[core], coef.at[core], coef_send.at[REACH], coef_recv.at[REACH], sibling, 0)
     share.start()
     share.wait_recv()
     for p in range(-REACH, REACH + 1):
         i = p + REACH
-        position = at(p)
-        factors = seven(
-            coef[1, i, 1], coef[0, i, 0], coef[0, i, 1], coef[1, i, 0], 0.5,
-            jnp.where(position == 0, 0.0, one), jnp.where(position == ns - 1, 0.0, one),
-        )
+        factors = seven(coef[1, i, 1], coef[0, i, 0], coef[0, i, 1], coef[1, i, 0], 0.5)
         for n in range(7):
             kap[n, i] = factors[n]
 
@@ -252,9 +314,9 @@
     def _():
         finish(w_ref[...])
 
-    for copy in halo0 + halo_c + halo1:
-        copy.wait_send()
-    pltpu.make_async_copy(some, some, coef_send.at[0]).wait()
+    for pair in (halo0, halo_c, halo1):
+        beside_do(pair, "send")
+    around(coef_send, True)
     share.wait_send()
     for i, j in enumerate(NEAR):
         sent(i, j, near[i])
@@ -277,7 +339,7 @@
         ended, delta = pl.pallas_call(
             lambda *refs: kernel(nt, ns, *refs),
             out_shape=(jax.ShapeDtypeStruct(fine, jnp.float32), jax.ShapeDtypeStruct(plane, jnp.float32)),
-            in_specs=[pl.BlockSpec(memory_space=pl.ANY)] * 3,
+            in_specs=[pl.BlockSpec(memory_space=pltpu.HBM)] * 3,
             out_specs=(pl.BlockSpec(memory_space=pltpu.VMEM),) * 2,
             scratch_shapes=[
                 vmem(*fine), vmem(3, *fine), vmem(*fine), vmem(2, cy, cz // 2),
@@ -286,10 +348,11 @@
                 vmem(2, 2 * REACH + 1, 2, *small), vmem(7, 2 * REACH + 1, *small),
                 vmem(*small), vmem(*small), vmem(*small),
                 *(vmem(2 * j + 1, *small) for j in NEAR), vmem(2 * MID + 1, *small), vmem(2 * FAR + 1, *small),
-                dma((3,)), dma((6,)), dma((6,)), dma((2,)), dma((2,)), dma((5,)), dma((5,)),
+                dma((3,)), dma((6,)), dma((6,)), dma((2 * REACH + 1,)), dma((2 * REACH + 1,)),
+                dma((5, 2 * FAR + 1)), dma((5, 2 * FAR + 1)),
                 pltpu.SemaphoreType.REGULAR((5,)),
             ],
-            compiler_params=pltpu.CompilerParams(collective_id=0, has_side_effects=True),
+            compiler_params=pltpu.CompilerParams(collective_id=0, has_side_effects=True, vmem_limit_bytes=56475648),
         )(initial_states, velocity, diffusivity)
         return (ended + delta[None])[None]
 

time: 42.2 us -> 42.7 us (1.012)
  Pallas kernels: 40.5 us -> 41.1 us
    pallas_call x1, Pallas kernels: 40.5 us -> 41.1 us  [shards(): pl.pallas_call(lambda *refs: kernel(nt, ns, *refs), out_shape=(jax.ShapeD...]
where the time goes in v2:
time: 42.7 us; the launch traced here: 42.5 us
  Pallas kernels  41.1 us (96%)
  other arithmetic  1.48 us (3%)
    pallas_call x1, Pallas kernels, shards(): pl.pallas_call(lambda *refs: kernel(nt, ns, *refs), out_shape=(jax.ShapeD...  41.1 us
    broadcast_in_dim x1, other arithmetic, shards(): return (ended + delta[None])[None]  1.48 us

profile of v2, /device:TPU:31, one launch (start us, length us, event | category | flops | bytes accessed | tf_op | source)
XLA Modules:
  0.0 42.5 jit_solution(6202353741007177961)
XLA Ops:
  0.0 41.1 %shard_map.37 = (f32[2,32,256]{2,1,0:T(8,128)}, f32[32,256]{1,0:T(8,128)S(1)}) custom-call(f32[1,2,32,256]{3,2,1,0:T(8,128)} %refs_0_.1, f32[3,2,32,256]{3,2,1,0:T(8,128)} %refs_1_.1, f32[2,32,256]{2,1,0:T(8,128)} %refs_2_.1), custom_call_target="tpu_custom_call" | custom-call | tf_op jit(solution)/shard_map/pallas_call | solution.py:339
  41.1 1.5 %add_bitcast_fusion = f32[1,2,32,256]{3,2,1,0:T(8,128)} fusion(f32[2,32,256]{2,1,0:T(8,128)} %get-tuple-element.7, f32[32,256]{1,0:T(8,128)S(1)} %get-tuple-element.8), kind=kLoop, calls=%fused_computation | loop fusion | flops 16384 | bytes 163840 | tf_op jit(solution)/shard_map/broadcast_in_dim | solution.py:357

commit v3 on v2

--- a/solution.py
+++ b/solution.py
@@ -9,6 +9,7 @@
 
 MESH = pl.DeviceIdType.MESH
 REACH = 7
+INNER = 3
 GREET = 8
 NEAR = (1, 2, 3)
 MID = 4
@@ -58,10 +59,10 @@
 
 def kernel(
     nt, ns, init, vel, dif, fine_out, delta_out,
-    f_ref, v_ref, k_ref, work, left0, right0, left1, right1, mid1,
+    f_ref, v_ref, k_ref, work, left0, right0, left1, right1, out_low, out_high,
     start_own, start_left, start_right, coef, kap,
     r_ref, u_ref, w_ref, near1, near2, near3, mid, far,
-    load_sem, halo_send, halo_recv, coef_send, coef_recv, hop_send, hop_recv, ready,
+    load_sem, halo_send, halo_recv, coef_send, coef_recv, share_send, share_recv, hop_send, hop_recv, ready,
 ):
     t, s = lax.axis_index("tm"), lax.axis_index("space")
     core = lax.rem(t, 2)
@@ -115,6 +116,18 @@
     ]
     for copy in loads:
         copy.start()
+    for copy in loads:
+        copy.wait()
+    fine0 = seven(k_ref[0], v_ref[0, 0], v_ref[1, 0], v_ref[2, 0], 1.0)
+    fine1 = seven(k_ref[1], v_ref[0, 1], v_ref[1, 1], v_ref[2, 1], 1.0)
+
+    def partial(a, b):
+        return inplane(fine0, a) + fine0[2] * b, inplane(fine1, b) + fine1[1] * a
+
+    pa, pb = partial(f_ref[0], f_ref[1])
+    out_low[0], out_low[1] = fine0[1], pa
+    out_high[0], out_high[1] = fine1[2], pb
+
     senders = sum(jnp.where(t >= j, 1, 0) for j in NEAR + (MID, FAR))
     beside = jnp.minimum(s, GREET) + jnp.minimum(ns - 1 - s, GREET)
     pl.semaphore_wait(barrier, beside + 1 + senders)
@@ -145,12 +158,16 @@
             else:
                 up.wait_send()
 
-    loads[0].wait()
     halo0 = [
         remote(f_ref.at[0], right0, halo_send.at[0], halo_recv.at[0], t, -1),
         remote(f_ref.at[1], left0, halo_send.at[1], halo_recv.at[1], t, 1),
     ]
+    halo1 = [
+        remote(out_low, right1, halo_send.at[4], halo_recv.at[4], t, -1),
+        remote(out_high, left1, halo_send.at[5], halo_recv.at[5], t, 1),
+    ]
     beside_do(halo0, "start")
+    beside_do(halo1, "start")
 
     for i, j in enumerate(NEAR + (MID, FAR)):
 
@@ -166,43 +183,30 @@
     ]
     beside_do(halo_c, "start")
 
-    loads[1].wait()
-    loads[2].wait()
     coarse = [restrict(work, v_ref[0]), restrict(work, v_ref[1]), restrict(work, v_ref[2]), restrict(work, k_ref)]
     for i in range(2):
         coef[core, REACH, i] = jnp.where(core == 0, coarse[i], coarse[2 + i])
-    for ds in reversed(outward(REACH)):
-
-        @pl.when(inside(ds))
-        def _():
-            i = REACH - ds
-            remote(coef.at[core, REACH], coef.at[core, i], coef_send.at[i], coef_recv.at[i], t, ds).start()
-
+    def spread(offsets):
+        for ds in offsets:
+
+            @pl.when(inside(ds))
+            def _():
+                i = REACH - ds
+                remote(coef.at[core, REACH], coef.at[core, i], coef_send.at[i], coef_recv.at[i], t, ds).start()
+
+    spread(reversed(outward(INNER)))
 
     one = jnp.float32(1.0)
-    fine0 = seven(k_ref[0], v_ref[0, 0], v_ref[1, 0], v_ref[2, 0], 1.0)
-    fine1 = seven(k_ref[1], v_ref[0, 1], v_ref[1, 1], v_ref[2, 1], 1.0)
-
-    def partial(a, b):
-        return inplane(fine0, a) + fine0[2] * b, inplane(fine1, b) + fine1[1] * a
-
-    pa, pb = partial(f_ref[0], f_ref[1])
-    beside_do(halo0, "recv")
-    mid1[0] = pa + fine0[1] * left0[...]
-    mid1[1] = pb + fine1[2] * right0[...]
-    halo1 = [
-        remote(mid1.at[0], right1, halo_send.at[4], halo_recv.at[4], t, -1),
-        remote(mid1.at[1], left1, halo_send.at[5], halo_recv.at[5], t, 1),
-    ]
-    beside_do(halo1, "start")
-
-    pa, pb = partial(mid1[0], mid1[1])
     own = seven(coarse[3], coarse[0], coarse[1], coarse[2], 0.5)
     beside_do(halo_c, "recv")
     stepped = inplane(own, start) + (own[1] * start_left[...] + own[2] * start_right[...])
+    beside_do(halo0, "recv")
+    a = pa + fine0[1] * left0[...]
+    b = pb + fine1[2] * right0[...]
+    pa, pb = partial(a, b)
     beside_do(halo1, "recv")
-    fine_out[0] = pa + fine0[1] * left1[...]
-    fine_out[1] = pb + fine1[2] * right1[...]
+    fine_out[0] = pa + fine0[1] * (left1[1] + left1[0] * f_ref[0])
+    fine_out[1] = pb + fine1[2] * (right1[1] + right1[0] * f_ref[1])
     end = restrict(work, fine_out)
     r_ref[...] = end - jnp.where(t == 0, 0.0, one) * stepped
 
@@ -243,8 +247,8 @@
     for i, j in enumerate(NEAR):
         hop(i, j, r_ref, near[i])
 
-    def around(sem, mirrored):
-        low, high = jnp.minimum(s, REACH), jnp.minimum(ns - 1 - s, REACH)
+    def around(sem, mirrored, first, last):
+        low, high = jnp.minimum(s, last), jnp.minimum(ns - 1 - s, last)
         if mirrored:
             low, high = high, low
 
@@ -252,18 +256,31 @@
             pltpu.make_async_copy(coef.at[core, i], coef.at[core, i], sem.at[i]).wait()
             return 0
 
-        lax.fori_loop(REACH - low, REACH, one_of, 0)
-        lax.fori_loop(REACH + 1, REACH + high + 1, one_of, 0)
-
-    around(coef_recv, False)
-    share = remote(coef.at[core], coef.at[core], coef_send.at[REACH], coef_recv.at[REACH], sibling, 0)
-    share.start()
-    share.wait_recv()
-    for p in range(-REACH, REACH + 1):
-        i = p + REACH
-        factors = seven(coef[1, i, 1], coef[0, i, 0], coef[0, i, 1], coef[1, i, 0], 0.5)
-        for n in range(7):
-            kap[n, i] = factors[n]
+        lax.fori_loop(REACH - low, REACH - first + 1, one_of, 0)
+        lax.fori_loop(REACH + first, REACH + high + 1, one_of, 0)
+
+    def share(number, first, last):
+        planes = coef.at[core, first:last]
+        return remote(planes, planes, share_send.at[number], share_recv.at[number], sibling, 0)
+
+    def factors_of(first, last):
+        for i in range(first, last):
+            factors = seven(coef[1, i, 1], coef[0, i, 0], coef[0, i, 1], coef[1, i, 0], 0.5)
+            for n in range(7):
+                kap[n, i] = factors[n]
+
+    low, high = REACH - INNER, REACH + INNER + 1
+    around(coef_recv, False, 1, INNER)
+    inner = share(0, low, high)
+    inner.start()
+    outer = [share(1, 0, low), share(2, high, 2 * REACH + 1)]
+
+    @pl.when(t >= FAR)
+    def _():
+        spread(reversed(outward(REACH)[: 2 * (REACH - INNER)]))
+
+    inner.wait_recv()
+    factors_of(low, high)
 
     def coarse_step(v):
         w = (v.shape[0] - 3) // 2
@@ -292,6 +309,17 @@
         w_ref[...] = u_ref[...]
 
     hop(4, FAR, w_ref, far)
+
+    @pl.when(t >= FAR)
+    def _():
+        around(coef_recv, False, INNER + 1, REACH)
+        for copy in outer:
+            copy.start()
+        for copy in outer:
+            copy.wait_recv()
+        factors_of(0, low)
+        factors_of(high, 2 * REACH + 1)
+
     arrived(4, FAR, far)
 
     def finish(c):
@@ -316,8 +344,15 @@
 
     for pair in (halo0, halo_c, halo1):
         beside_do(pair, "send")
-    around(coef_send, True)
-    share.wait_send()
+    around(coef_send, True, 1, INNER)
+    inner.wait_send()
+
+    @pl.when(t >= FAR)
+    def _():
+        around(coef_send, True, INNER + 1, REACH)
+        for copy in outer:
+            copy.wait_send()
+
     for i, j in enumerate(NEAR):
         sent(i, j, near[i])
     sent(3, MID, mid)
@@ -343,16 +378,16 @@
             out_specs=(pl.BlockSpec(memory_space=pltpu.VMEM),) * 2,
             scratch_shapes=[
                 vmem(*fine), vmem(3, *fine), vmem(*fine), vmem(2, cy, cz // 2),
-                vmem(*plane), vmem(*plane), vmem(*plane), vmem(*plane), vmem(*fine),
+                vmem(*plane), vmem(*plane), vmem(*fine), vmem(*fine), vmem(*fine), vmem(*fine),
                 vmem(*small), vmem(*small), vmem(*small),
                 vmem(2, 2 * REACH + 1, 2, *small), vmem(7, 2 * REACH + 1, *small),
                 vmem(*small), vmem(*small), vmem(*small),
                 *(vmem(2 * j + 1, *small) for j in NEAR), vmem(2 * MID + 1, *small), vmem(2 * FAR + 1, *small),
-                dma((3,)), dma((6,)), dma((6,)), dma((2 * REACH + 1,)), dma((2 * REACH + 1,)),
+                dma((3,)), dma((6,)), dma((6,)), dma((2 * REACH + 1,)), dma((2 * REACH + 1,)), dma((3,)), dma((3,)),
                 dma((5, 2 * FAR + 1)), dma((5, 2 * FAR + 1)),
                 pltpu.SemaphoreType.REGULAR((5,)),
             ],
-            compiler_params=pltpu.CompilerParams(collective_id=0, has_side_effects=True, vmem_limit_bytes=56475648),
+            compiler_params=pltpu.CompilerParams(collective_id=0, has_side_effects=True, vmem_limit_bytes=56430000),
         )(initial_states, velocity, diffusivity)
         return (ended + delta[None])[None]
 

time: 42.7 us -> 39.6 us (0.927); the launches traced: 42.5 us -> 38.8 us
  Pallas kernels: 41.1 us -> 38.2 us
  other arithmetic: 1.48 us -> 0.64 us
    pallas_call x1, Pallas kernels: 41.1 us -> 38.2 us  [shards(): pl.pallas_call(lambda *refs: kernel(nt, ns, *refs), out_shape=(jax.ShapeD...]
    broadcast_in_dim x1, other arithmetic: 1.48 us -> 0.64 us  [shards(): return (ended + delta[None])[None]]
where the time goes in v3:
time: 39.6 us; the launch traced here: 38.8 us
  Pallas kernels  38.2 us (96%)
  other arithmetic  0.64 us (2%)
    pallas_call x1, Pallas kernels, shards(): pl.pallas_call(lambda *refs: kernel(nt, ns, *refs), out_shape=(jax.ShapeD...  38.2 us

profile of v3, /device:TPU:31, one launch (start us, length us, event | category | flops | bytes accessed | tf_op | source)
XLA Modules:
  0.0 38.8 jit_solution(6643637986740835603)
XLA Ops:
  0.0 38.2 %shard_map.37 = (f32[2,32,256]{2,1,0:T(8,128)S(1)}, f32[32,256]{1,0:T(8,128)S(1)}) custom-call(f32[1,2,32,256]{3,2,1,0:T(8,128)} %refs_0_.1, f32[3,2,32,256]{3,2,1,0:T(8,128)} %refs_1_.1, f32[2,32,256]{2,1,0:T(8,128)} %refs_2_.1), custom_call_target="tpu_custom_call" | custom-call | tf_op jit(solution)/shard_map/pallas_call | solution.py:374
  38.2 0.6 %add_bitcast_fusion = f32[1,2,32,256]{3,2,1,0:T(8,128)} fusion(f32[2,32,256]{2,1,0:T(8,128)S(1)} %get-tuple-element.7, f32[32,256]{1,0:T(8,128)S(1)} %get-tuple-element.8), kind=kLoop, calls=%fused_computation | loop fusion | flops 16384 | bytes 163840 | tf_op jit(solution)/shard_map/broadcast_in_dim | solution.py:392

commit v4 on v3

--- a/solution.py
+++ b/solution.py
@@ -10,10 +10,11 @@
 MESH = pl.DeviceIdType.MESH
 REACH = 7
 INNER = 3
-GREET = 8
+GREET = 4
 NEAR = (1, 2, 3)
 MID = 4
 FAR = 8
+HOPS = NEAR + (MID, FAR)
 
 
 def seven(diffusivity, vx, vy, vz, spread):
@@ -62,11 +63,11 @@
     f_ref, v_ref, k_ref, work, left0, right0, left1, right1, out_low, out_high,
     start_own, start_left, start_right, coef, kap,
     r_ref, u_ref, w_ref, near1, near2, near3, mid, far,
-    load_sem, halo_send, halo_recv, coef_send, coef_recv, share_send, share_recv, hop_send, hop_recv, ready,
+    load_sem, halo_send, halo_recv, coef_send, coef_recv, share_send, hop_send, hop_recv, ready,
 ):
     t, s = lax.axis_index("tm"), lax.axis_index("space")
-    core = lax.rem(t, 2)
-    sibling = t + 1 - 2 * core
+    seat = lax.rem(t, FAR)
+    group = t - seat
     near = (near1, near2, near3)
 
     def inside(ds):
@@ -103,10 +104,9 @@
         def _():
             pl.semaphore_signal(barrier, inc=1, device_id=(t, s + ds), device_id_type=MESH)
 
-    pl.semaphore_signal(barrier, inc=1, device_id=(sibling, s), device_id_type=MESH)
-    for j in NEAR + (MID, FAR):
-
-        @pl.when(t + j < nt)
+    for j in range(1, FAR + 1):
+
+        @pl.when((t + j < nt) if j in HOPS else (seat + j < FAR))
         def _():
             pl.semaphore_signal(barrier, inc=1, device_id=(t + j, s), device_id_type=MESH)
 
@@ -128,9 +128,16 @@
     out_low[0], out_low[1] = fine0[1], pa
     out_high[0], out_high[1] = fine1[2], pb
 
-    senders = sum(jnp.where(t >= j, 1, 0) for j in NEAR + (MID, FAR))
+    start = restrict(work.at[0], f_ref)
+    start_own[...] = start
+    coarse = [restrict(work.at[1 + i], v_ref[i]) for i in range(3)]
+    coarse.append(restrict(work.at[4], k_ref))
+    for i in range(4):
+        coef[REACH, i] = coarse[i]
+
+    senders = sum(jnp.where((t if j in HOPS else seat) >= j, 1, 0) for j in range(1, FAR + 1))
     beside = jnp.minimum(s, GREET) + jnp.minimum(ns - 1 - s, GREET)
-    pl.semaphore_wait(barrier, beside + 1 + senders)
+    pl.semaphore_wait(barrier, beside + senders)
 
     def remote(src, dst, send, recv, tt, ds):
         return pltpu.make_async_remote_copy(
@@ -166,35 +173,87 @@
         remote(out_low, right1, halo_send.at[4], halo_recv.at[4], t, -1),
         remote(out_high, left1, halo_send.at[5], halo_recv.at[5], t, 1),
     ]
-    beside_do(halo0, "start")
-    beside_do(halo1, "start")
-
-    for i, j in enumerate(NEAR + (MID, FAR)):
-
-        @pl.when(t >= j)
-        def _():
-            pl.semaphore_signal(ready.at[i], inc=1, device_id=(t - j, s), device_id_type=MESH)
-
-    start = restrict(work, f_ref)
-    start_own[...] = start
     halo_c = [
         remote(start_own, start_right, halo_send.at[2], halo_recv.at[2], t, -1),
         remote(start_own, start_left, halo_send.at[3], halo_recv.at[3], t, 1),
     ]
+    def reach(off):
+        return (s + off >= 0) & (s + off < ns)
+
+    inner = (seat < 2 * INNER, jnp.where(seat < INNER, seat - INNER, seat - INNER + 1))
+    outer = (group > 0, jnp.where(seat < REACH - INNER, seat - REACH, seat))
+
+    def fetch(who, i):
+        needed, off = who
+
+        @pl.when(needed & reach(-off))
+        def _():
+            there = REACH + off
+            remote(coef.at[REACH], coef.at[there], coef_send.at[i], coef_recv.at[there], t, -off).start()
+
+    def fetched(who, i):
+        needed, off = who
+
+        @pl.when(needed & reach(-off))
+        def _():
+            pltpu.make_async_copy(coef.at[REACH], coef.at[REACH], coef_send.at[i]).wait()
+
+    def hand_on(who, i):
+        needed, off = who
+
+        @pl.when(needed & reach(off))
+        def _():
+            here = REACH + off
+            pltpu.make_async_copy(coef.at[here], coef.at[here], coef_recv.at[here]).wait()
+            for turn in (4, 3, 5, 2, 6, 1, 7):
+                to = group + lax.rem(seat + turn, FAR)
+                remote(coef.at[here], coef.at[here], share_send.at[i, turn], coef_recv.at[here], to, 0).start()
+
+    def handed_on(who, i):
+        needed, off = who
+
+        @pl.when(needed & reach(off))
+        def _():
+            for turn in range(1, FAR):
+                pltpu.make_async_copy(coef.at[REACH], coef.at[REACH], share_send.at[i, turn]).wait()
+
+    def handed(who, offs):
+        needed, off = who
+        for o in offs:
+
+            @pl.when(inside(o) & (jnp.logical_not(needed) | (off != o)))
+            def _():
+                pltpu.make_async_copy(coef.at[REACH + o], coef.at[REACH + o], coef_recv.at[REACH + o]).wait()
+
+    beside_do(halo0, "start")
+    fetch(inner, 0)
+    beside_do(halo1, "start")
     beside_do(halo_c, "start")
-
-    coarse = [restrict(work, v_ref[0]), restrict(work, v_ref[1]), restrict(work, v_ref[2]), restrict(work, k_ref)]
-    for i in range(2):
-        coef[core, REACH, i] = jnp.where(core == 0, coarse[i], coarse[2 + i])
-    def spread(offsets):
-        for ds in offsets:
+    for i, j in enumerate(HOPS[:-1]):
+
+        @pl.when(t >= j)
+        def _():
+            pl.semaphore_signal(ready.at[i], inc=1, device_id=(t - j, s), device_id_type=MESH)
+
+    for j in range(1, FAR):
+
+        @pl.when(seat >= j)
+        def _():
+            pl.semaphore_signal(ready.at[5], inc=1, device_id=(t - j, s), device_id_type=MESH)
+
+    @pl.when(seat < FAR - 1)
+    def _():
+        pl.semaphore_wait(ready.at[5], FAR - 1 - seat)
+
+    @pl.when(group > 0)
+    def _():
+        for ds in (GREET, -GREET):
 
             @pl.when(inside(ds))
             def _():
-                i = REACH - ds
-                remote(coef.at[core, REACH], coef.at[core, i], coef_send.at[i], coef_recv.at[i], t, ds).start()
-
-    spread(reversed(outward(INNER)))
+                pl.semaphore_signal(ready.at[6], inc=1, device_id=(t, s + ds), device_id_type=MESH)
+
+    hand_on(inner, 0)
 
     one = jnp.float32(1.0)
     own = seven(coarse[3], coarse[0], coarse[1], coarse[2], 0.5)
@@ -207,7 +266,7 @@
     beside_do(halo1, "recv")
     fine_out[0] = pa + fine0[1] * (left1[1] + left1[0] * f_ref[0])
     fine_out[1] = pb + fine1[2] * (right1[1] + right1[0] * f_ref[1])
-    end = restrict(work, fine_out)
+    end = restrict(work.at[0], fine_out)
     r_ref[...] = end - jnp.where(t == 0, 0.0, one) * stepped
 
     def each(width, slot, sem, mirrored):
@@ -247,39 +306,20 @@
     for i, j in enumerate(NEAR):
         hop(i, j, r_ref, near[i])
 
-    def around(sem, mirrored, first, last):
-        low, high = jnp.minimum(s, last), jnp.minimum(ns - 1 - s, last)
-        if mirrored:
-            low, high = high, low
-
-        def one_of(i, _):
-            pltpu.make_async_copy(coef.at[core, i], coef.at[core, i], sem.at[i]).wait()
-            return 0
-
-        lax.fori_loop(REACH - low, REACH - first + 1, one_of, 0)
-        lax.fori_loop(REACH + first, REACH + high + 1, one_of, 0)
-
-    def share(number, first, last):
-        planes = coef.at[core, first:last]
-        return remote(planes, planes, share_send.at[number], share_recv.at[number], sibling, 0)
-
     def factors_of(first, last):
         for i in range(first, last):
-            factors = seven(coef[1, i, 1], coef[0, i, 0], coef[0, i, 1], coef[1, i, 0], 0.5)
+            factors = seven(coef[i, 3], coef[i, 0], coef[i, 1], coef[i, 2], 0.5)
             for n in range(7):
                 kap[n, i] = factors[n]
 
     low, high = REACH - INNER, REACH + INNER + 1
-    around(coef_recv, False, 1, INNER)
-    inner = share(0, low, high)
-    inner.start()
-    outer = [share(1, 0, low), share(2, high, 2 * REACH + 1)]
-
-    @pl.when(t >= FAR)
-    def _():
-        spread(reversed(outward(REACH)[: 2 * (REACH - INNER)]))
-
-    inner.wait_recv()
+    @pl.when(group > 0)
+    def _():
+        pl.semaphore_wait(ready.at[6], jnp.where(inside(GREET), 1, 0) + jnp.where(inside(-GREET), 1, 0))
+        pl.semaphore_signal(ready.at[len(HOPS) - 1], inc=1, device_id=(t - FAR, s), device_id_type=MESH)
+
+    fetch(outer, 1)
+    handed(inner, [o for o in range(-INNER, INNER + 1) if o])
     factors_of(low, high)
 
     def coarse_step(v):
@@ -295,6 +335,7 @@
     u_ref[...] = coarse_step(v)[0] + r_ref[...]
 
     hop(3, MID, u_ref, mid)
+    hand_on(outer, 1)
     arrived(3, MID, mid)
 
     @pl.when(t >= MID)
@@ -310,13 +351,19 @@
 
     hop(4, FAR, w_ref, far)
 
+    for pair in (halo0, halo_c, halo1):
+        beside_do(pair, "send")
+    fetched(inner, 0)
+    fetched(outer, 1)
+    handed_on(inner, 0)
+    handed_on(outer, 1)
+    for i, j in enumerate(NEAR):
+        sent(i, j, near[i])
+    sent(3, MID, mid)
+
     @pl.when(t >= FAR)
     def _():
-        around(coef_recv, False, INNER + 1, REACH)
-        for copy in outer:
-            copy.start()
-        for copy in outer:
-            copy.wait_recv()
+        handed(outer, [o for o in range(-REACH, REACH + 1) if abs(o) > INNER])
         factors_of(0, low)
         factors_of(high, 2 * REACH + 1)
 
@@ -328,8 +375,8 @@
         for h in range(2):
             wide = jnp.take_along_axis(d, lanes // 2 + 64 * h, axis=1)
             for i in range(2):
-                work[h, pl.ds(i, d.shape[0], 2), :] = wide
-            delta_out[:, 128 * h : 128 * (h + 1)] = work[h]
+                work[0, h, pl.ds(i, d.shape[0], 2), :] = wide
+            delta_out[:, 128 * h : 128 * (h + 1)] = work[0, h]
 
     @pl.when(t >= FAR)
     def _():
@@ -342,20 +389,6 @@
     def _():
         finish(w_ref[...])
 
-    for pair in (halo0, halo_c, halo1):
-        beside_do(pair, "send")
-    around(coef_send, True, 1, INNER)
-    inner.wait_send()
-
-    @pl.when(t >= FAR)
-    def _():
-        around(coef_send, True, INNER + 1, REACH)
-        for copy in outer:
-            copy.wait_send()
-
-    for i, j in enumerate(NEAR):
-        sent(i, j, near[i])
-    sent(3, MID, mid)
     sent(4, FAR, far)
 
 
@@ -377,15 +410,15 @@
             in_specs=[pl.BlockSpec(memory_space=pltpu.HBM)] * 3,
             out_specs=(pl.BlockSpec(memory_space=pltpu.VMEM),) * 2,
             scratch_shapes=[
-                vmem(*fine), vmem(3, *fine), vmem(*fine), vmem(2, cy, cz // 2),
+                vmem(*fine), vmem(3, *fine), vmem(*fine), vmem(5, 2, cy, cz // 2),
                 vmem(*plane), vmem(*plane), vmem(*fine), vmem(*fine), vmem(*fine), vmem(*fine),
                 vmem(*small), vmem(*small), vmem(*small),
-                vmem(2, 2 * REACH + 1, 2, *small), vmem(7, 2 * REACH + 1, *small),
+                vmem(2 * REACH + 1, 4, *small), vmem(7, 2 * REACH + 1, *small),
                 vmem(*small), vmem(*small), vmem(*small),
                 *(vmem(2 * j + 1, *small) for j in NEAR), vmem(2 * MID + 1, *small), vmem(2 * FAR + 1, *small),
-                dma((3,)), dma((6,)), dma((6,)), dma((2 * REACH + 1,)), dma((2 * REACH + 1,)), dma((3,)), dma((3,)),
+                dma((3,)), dma((6,)), dma((6,)), dma((2,)), dma((2 * REACH + 1,)), dma((2, FAR)),
                 dma((5, 2 * FAR + 1)), dma((5, 2 * FAR + 1)),
-                pltpu.SemaphoreType.REGULAR((5,)),
+                pltpu.SemaphoreType.REGULAR((7,)),
             ],
             compiler_params=pltpu.CompilerParams(collective_id=0, has_side_effects=True, vmem_limit_bytes=56430000),
         )(initial_states, velocity, diffusivity)

time: 39.6 us -> 36 us (0.909)
  the two profiles are of different devices: /device:TPU:31 before, /device:TPU:30 now
where the time goes in v4:
time: 36 us; the launch traced here: 35.8 us
  Pallas kernels  35.2 us (98%)
  other arithmetic  0.64 us (2%)
    pallas_call x1, Pallas kernels, shards(): pl.pallas_call(lambda *refs: kernel(nt, ns, *refs), out_shape=(jax.ShapeD...  35.2 us

profile of v4, /device:TPU:30, one launch (start us, length us, event | category | flops | bytes accessed | tf_op | source)
XLA Modules:
  0.0 35.8 jit_solution(16541274931865222257)
XLA Ops:
  0.0 35.2 %shard_map.37 = (f32[2,32,256]{2,1,0:T(8,128)S(1)}, f32[32,256]{1,0:T(8,128)S(1)}) custom-call(f32[1,2,32,256]{3,2,1,0:T(8,128)} %refs_0_.1, f32[3,2,32,256]{3,2,1,0:T(8,128)} %refs_1_.1, f32[2,32,256]{2,1,0:T(8,128)} %refs_2_.1), custom_call_target="tpu_custom_call" | custom-call | tf_op jit(solution)/shard_map/pallas_call | solution.py:407
  35.2 0.6 %add_bitcast_fusion = f32[1,2,32,256]{3,2,1,0:T(8,128)} fusion(f32[2,32,256]{2,1,0:T(8,128)S(1)} %get-tuple-element.7, f32[32,256]{1,0:T(8,128)S(1)} %get-tuple-element.8), kind=kLoop, calls=%fused_computation | loop fusion | flops 16384 | bytes 163840 | tf_op jit(solution)/shard_map/broadcast_in_dim | solution.py:425

commit v5 on v4

--- a/solution.py
+++ b/solution.py
@@ -10,7 +10,8 @@
 MESH = pl.DeviceIdType.MESH
 REACH = 7
 INNER = 3
-GREET = 4
+GREET = 2
+FOURTH = 4
 NEAR = (1, 2, 3)
 MID = 4
 FAR = 8
@@ -76,46 +77,47 @@
     def outward(width):
         return [ds for k in range(width, 0, -1) for ds in (k, -k)]
 
-    for j, slot in zip(NEAR, near):
-
-        @pl.when(t < j)
-        def _():
-            slot[...] = jnp.zeros_like(slot)
-
-    @pl.when((s < FAR) | (s >= ns - FAR))
-    def _():
-        for slot in (near1, near2, near3, mid, far, coef):
-            slot[...] = jnp.zeros_like(slot)
-
-    @pl.when(s == 0)
-    def _():
-        for slot in (left0, left1, start_left):
-            slot[...] = jnp.zeros_like(slot)
-
-    @pl.when(s == ns - 1)
-    def _():
-        for slot in (right0, right1, start_right):
-            slot[...] = jnp.zeros_like(slot)
-
-    barrier = pltpu.get_barrier_semaphore()
-    for ds in reversed(outward(GREET)):
-
-        @pl.when(inside(ds))
-        def _():
-            pl.semaphore_signal(barrier, inc=1, device_id=(t, s + ds), device_id_type=MESH)
-
-    for j in range(1, FAR + 1):
-
-        @pl.when((t + j < nt) if j in HOPS else (seat + j < FAR))
-        def _():
-            pl.semaphore_signal(barrier, inc=1, device_id=(t + j, s), device_id_type=MESH)
-
     loads = [
         pltpu.make_async_copy(a, b, load_sem.at[i])
         for i, (a, b) in enumerate(((init.at[0], f_ref), (vel, v_ref), (dif, k_ref)))
     ]
     for copy in loads:
         copy.start()
+
+    for j, slot in zip(NEAR, near):
+
+        @pl.when(t < j)
+        def _():
+            slot[...] = jnp.zeros_like(slot)
+
+    @pl.when((s < FAR) | (s >= ns - FAR))
+    def _():
+        for slot in (near1, near2, near3, mid, far, coef):
+            slot[...] = jnp.zeros_like(slot)
+
+    @pl.when(s == 0)
+    def _():
+        for slot in (left0, left1, start_left):
+            slot[...] = jnp.zeros_like(slot)
+
+    @pl.when(s == ns - 1)
+    def _():
+        for slot in (right0, right1, start_right):
+            slot[...] = jnp.zeros_like(slot)
+
+    barrier = pltpu.get_barrier_semaphore()
+    for ds in reversed(outward(GREET)):
+
+        @pl.when(inside(ds))
+        def _():
+            pl.semaphore_signal(barrier, inc=1, device_id=(t, s + ds), device_id_type=MESH)
+
+    for j in range(1, FAR + 1):
+
+        @pl.when((t + j < nt) if j in HOPS else (seat + j < FAR))
+        def _():
+            pl.semaphore_signal(barrier, inc=1, device_id=(t + j, s), device_id_type=MESH)
+
     for copy in loads:
         copy.wait()
     fine0 = seven(k_ref[0], v_ref[0, 0], v_ref[1, 0], v_ref[2, 0], 1.0)
@@ -180,7 +182,10 @@
     def reach(off):
         return (s + off >= 0) & (s + off < ns)
 
-    inner = (seat < 2 * INNER, jnp.where(seat < INNER, seat - INNER, seat - INNER + 1))
+    near_off = jnp.where(seat < GREET, seat - GREET, seat - GREET + 1)
+    inner = (seat < 2 * INNER, jnp.where(seat < 2 * GREET, near_off, jnp.where(seat == 2 * GREET, -INNER, INNER)))
+    inner_first = (seat < 2 * GREET, inner[1])
+    inner_last = ((seat >= 2 * GREET) & (seat < 2 * INNER), inner[1])
     outer = (group > 0, jnp.where(seat < REACH - INNER, seat - REACH, seat))
 
     def fetch(who, i):
@@ -226,32 +231,47 @@
                 pltpu.make_async_copy(coef.at[REACH + o], coef.at[REACH + o], coef_recv.at[REACH + o]).wait()
 
     beside_do(halo0, "start")
-    fetch(inner, 0)
+    fetch(inner_first, 0)
     beside_do(halo1, "start")
     beside_do(halo_c, "start")
-    for i, j in enumerate(HOPS[:-1]):
-
+    def tell(i, j):
         @pl.when(t >= j)
         def _():
             pl.semaphore_signal(ready.at[i], inc=1, device_id=(t - j, s), device_id_type=MESH)
 
-    for j in range(1, FAR):
-
-        @pl.when(seat >= j)
-        def _():
-            pl.semaphore_signal(ready.at[5], inc=1, device_id=(t - j, s), device_id_type=MESH)
-
-    @pl.when(seat < FAR - 1)
-    def _():
-        pl.semaphore_wait(ready.at[5], FAR - 1 - seat)
-
-    @pl.when(group > 0)
-    def _():
-        for ds in (GREET, -GREET):
+    def word(i, width):
+        for ds in (width, -width):
 
             @pl.when(inside(ds))
             def _():
-                pl.semaphore_signal(ready.at[6], inc=1, device_id=(t, s + ds), device_id_type=MESH)
+                pl.semaphore_signal(ready.at[i], inc=1, device_id=(t, s + ds), device_id_type=MESH)
+
+    def heard(i, width):
+        pl.semaphore_wait(ready.at[i], jnp.where(inside(width), 1, 0) + jnp.where(inside(-width), 1, 0))
+
+    word(7, GREET)
+    for i, j in enumerate(HOPS):
+        if j <= GREET:
+            tell(i, j)
+    for j in range(1, FAR):
+
+        @pl.when(seat >= j)
+        def _():
+            pl.semaphore_signal(ready.at[5], inc=1, device_id=(t - j, s), device_id_type=MESH)
+
+    heard(7, GREET)
+    fetch(inner_last, 0)
+    for i, j in enumerate(HOPS):
+        if GREET < j <= FOURTH:
+            tell(i, j)
+
+    @pl.when(group > 0)
+    def _():
+        word(6, FOURTH)
+
+    @pl.when(seat < FAR - 1)
+    def _():
+        pl.semaphore_wait(ready.at[5], FAR - 1 - seat)
 
     hand_on(inner, 0)
 
@@ -315,8 +335,8 @@
     low, high = REACH - INNER, REACH + INNER + 1
     @pl.when(group > 0)
     def _():
-        pl.semaphore_wait(ready.at[6], jnp.where(inside(GREET), 1, 0) + jnp.where(inside(-GREET), 1, 0))
-        pl.semaphore_signal(ready.at[len(HOPS) - 1], inc=1, device_id=(t - FAR, s), device_id_type=MESH)
+        heard(6, FOURTH)
+        tell(len(HOPS) - 1, FAR)
 
     fetch(outer, 1)
     handed(inner, [o for o in range(-INNER, INNER + 1) if o])
@@ -418,7 +438,7 @@
                 *(vmem(2 * j + 1, *small) for j in NEAR), vmem(2 * MID + 1, *small), vmem(2 * FAR + 1, *small),
                 dma((3,)), dma((6,)), dma((6,)), dma((2,)), dma((2 * REACH + 1,)), dma((2, FAR)),
                 dma((5, 2 * FAR + 1)), dma((5, 2 * FAR + 1)),
-                pltpu.SemaphoreType.REGULAR((7,)),
+                pltpu.SemaphoreType.REGULAR((8,)),
             ],
             compiler_params=pltpu.CompilerParams(collective_id=0, has_side_effects=True, vmem_limit_bytes=56430000),
         )(initial_states, velocity, diffusivity)

time: 36 us -> 34.7 us (0.964)
  the two profiles are of different devices: /device:TPU:30 before, /device:TPU:22 now
where the time goes in v5:
time: 34.7 us; the launch traced here: 34.6 us
  Pallas kernels  33.9 us (98%)
  other arithmetic  0.64 us (2%)
    pallas_call x1, Pallas kernels, shards(): pl.pallas_call(lambda *refs: kernel(nt, ns, *refs), out_shape=(jax.ShapeD...  33.9 us

profile of v5, /device:TPU:22, one launch (start us, length us, event | category | flops | bytes accessed | tf_op | source)
XLA Modules:
  0.0 34.6 jit_solution(12171604682666105739)
XLA Ops:
  0.0 33.9 %shard_map.37 = (f32[2,32,256]{2,1,0:T(8,128)S(1)}, f32[32,256]{1,0:T(8,128)S(1)}) custom-call(f32[1,2,32,256]{3,2,1,0:T(8,128)} %refs_0_.1, f32[3,2,32,256]{3,2,1,0:T(8,128)} %refs_1_.1, f32[2,32,256]{2,1,0:T(8,128)} %refs_2_.1), custom_call_target="tpu_custom_call" | custom-call | tf_op jit(solution)/shard_map/pallas_call | solution.py:427
  33.9 0.6 %add_bitcast_fusion = f32[1,2,32,256]{3,2,1,0:T(8,128)} fusion(f32[2,32,256]{2,1,0:T(8,128)S(1)} %get-tuple-element.7, f32[32,256]{1,0:T(8,128)S(1)} %get-tuple-element.8), kind=kLoop, calls=%fused_computation | loop fusion | flops 16384 | bytes 163840 | tf_op jit(solution)/shard_map/broadcast_in_dim | solution.py:445

commit v6 on v5

--- a/solution.py
+++ b/solution.py
@@ -273,7 +273,7 @@
     def _():
         pl.semaphore_wait(ready.at[5], FAR - 1 - seat)
 
-    hand_on(inner, 0)
+    hand_on(inner_first, 0)
 
     one = jnp.float32(1.0)
     own = seven(coarse[3], coarse[0], coarse[1], coarse[2], 0.5)
@@ -339,8 +339,9 @@
         tell(len(HOPS) - 1, FAR)
 
     fetch(outer, 1)
-    handed(inner, [o for o in range(-INNER, INNER + 1) if o])
-    factors_of(low, high)
+    hand_on(inner_last, 0)
+    handed(inner, [o for o in range(-GREET, GREET + 1) if o])
+    factors_of(low + 1, high - 1)
 
     def coarse_step(v):
         w = (v.shape[0] - 3) // 2
@@ -355,6 +356,9 @@
     u_ref[...] = coarse_step(v)[0] + r_ref[...]
 
     hop(3, MID, u_ref, mid)
+    handed(inner, [-INNER, INNER])
+    factors_of(low, low + 1)
+    factors_of(high - 1, high)
     hand_on(outer, 1)
     arrived(3, MID, mid)
 

time: 34.7 us -> 33.9 us (0.977)
  the two profiles are of different devices: /device:TPU:22 before, /device:TPU:94 now
where the time goes in v6:
time: 33.9 us; the launch traced here: 33.8 us
  Pallas kernels  33.1 us (98%)
  other arithmetic  0.64 us (2%)
    pallas_call x1, Pallas kernels, shards(): pl.pallas_call(lambda *refs: kernel(nt, ns, *refs), out_shape=(jax.ShapeD...  33.1 us

profile of v6, /device:TPU:94, one launch (start us, length us, event | category | flops | bytes accessed | tf_op | source)
XLA Modules:
  0.0 33.8 jit_solution(513468806049001724)
XLA Ops:
  0.0 33.1 %shard_map.37 = (f32[2,32,256]{2,1,0:T(8,128)S(1)}, f32[32,256]{1,0:T(8,128)S(1)}) custom-call(f32[1,2,32,256]{3,2,1,0:T(8,128)} %refs_0_.1, f32[3,2,32,256]{3,2,1,0:T(8,128)} %refs_1_.1, f32[2,32,256]{2,1,0:T(8,128)} %refs_2_.1), custom_call_target="tpu_custom_call" | custom-call | tf_op jit(solution)/shard_map/pallas_call | solution.py:431
  33.1 0.6 %add_bitcast_fusion = f32[1,2,32,256]{3,2,1,0:T(8,128)} fusion(f32[2,32,256]{2,1,0:T(8,128)S(1)} %get-tuple-element.7, f32[32,256]{1,0:T(8,128)S(1)} %get-tuple-element.8), kind=kLoop, calls=%fused_computation | loop fusion | flops 16384 | bytes 163840 | tf_op jit(solution)/shard_map/broadcast_in_dim | solution.py:449

commit v7 on v6

--- a/solution.py
+++ b/solution.py
@@ -230,10 +230,10 @@
             def _():
                 pltpu.make_async_copy(coef.at[REACH + o], coef.at[REACH + o], coef_recv.at[REACH + o]).wait()
 
+    beside_do(halo_c, "start")
+    fetch(inner_first, 0)
     beside_do(halo0, "start")
-    fetch(inner_first, 0)
     beside_do(halo1, "start")
-    beside_do(halo_c, "start")
     def tell(i, j):
         @pl.when(t >= j)
         def _():

time: 33.9 us -> 33.7 us (level)
  no operation moved by 1% of the time
where the time goes in v7:
time: 33.7 us; the launch traced here: 33.6 us
  Pallas kernels  33 us (98%)
  other arithmetic  0.64 us (2%)
    pallas_call x1, Pallas kernels, shards(): pl.pallas_call(lambda *refs: kernel(nt, ns, *refs), out_shape=(jax.ShapeD...  33 us

profile of v7, /device:TPU:94, one launch (start us, length us, event | category | flops | bytes accessed | tf_op | source)
XLA Modules:
  0.0 33.6 jit_solution(3533691854098953548)
XLA Ops:
  0.0 33.0 %shard_map.37 = (f32[2,32,256]{2,1,0:T(8,128)S(1)}, f32[32,256]{1,0:T(8,128)S(1)}) custom-call(f32[1,2,32,256]{3,2,1,0:T(8,128)} %refs_0_.1, f32[3,2,32,256]{3,2,1,0:T(8,128)} %refs_1_.1, f32[2,32,256]{2,1,0:T(8,128)} %refs_2_.1), custom_call_target="tpu_custom_call" | custom-call | tf_op jit(solution)/shard_map/pallas_call | solution.py:431
  33.0 0.6 %add_bitcast_fusion = f32[1,2,32,256]{3,2,1,0:T(8,128)} fusion(f32[2,32,256]{2,1,0:T(8,128)S(1)} %get-tuple-element.7, f32[32,256]{1,0:T(8,128)S(1)} %get-tuple-element.8), kind=kLoop, calls=%fused_computation | loop fusion | flops 16384 | bytes 163840 | tf_op jit(solution)/shard_map/broadcast_in_dim | solution.py:449
